TPU v7x, 32 devices: a whole 2x2x4 slice. The times are simulated.
32 devices in a mesh: dp: 8 (over y, x, core), tensor: 4 (over z).
Axes of the slice: x: 2, y: 2, z: 4, core: 2. Of those that a mesh axis runs over, the one named last changes fastest.
Arguments:
- block_input: bfloat16 [16, 2048, 768], P('dp', 'tensor'), may hold values from -6 to 6
- norm_gain: float32 [768], replicated, may hold values from 0.5 to 1.5
- input_gate_inner_weight: bfloat16 [768, 2, 1536], P('dp', None, 'tensor'), may hold values from -0.21875 to 0.21875
- input_shared_weight: bfloat16 [768, 256], P('dp'), may hold values from -0.21875 to 0.21875
- input_delta_weight: bfloat16 [768, 24], P('dp', 'tensor'), may hold values from -0.21875 to 0.21875
- conv_inner: bfloat16 [4, 1536], P(None, 'tensor'), may hold values from -3 to 3
- shift_inner: bfloat16 [1536], P('tensor'), may hold values from -3 to 3
- conv_shared: bfloat16 [4, 256], replicated, may hold values from -3 to 3
- shift_shared: bfloat16 [256], replicated, may hold values from -3 to 3
- decay_log: float32 [24], P('tensor'), may hold values from 0 to 2.77
- delta_bias: float32 [24], P('tensor'), may hold values from -6.9 to -2.3
- skip_gain: float32 [24], P('tensor'), may hold values from 0.5 to 1.5
- gated_gain: float32 [1536], P('tensor'), may hold values from 0.5 to 1.5
- output_projection_weight: bfloat16 [1536, 768], P('tensor', 'dp'), may hold values from -0.15625 to 0.15625
- cotangent: bfloat16 [16, 2048, 768], P('dp', 'tensor'), may hold values from -6 to 6
Outputs:
- block_output: bfloat16 [16, 2048, 768], P('dp', 'tensor')
- input_grad: bfloat16 [16, 2048, 768], P('dp', 'tensor')
- norm_gain_grad: float32 [768], replicated
- gate_inner_grad: float32 [768, 2, 1536], P('dp', None, 'tensor')
- shared_bc_grad: float32 [768, 256], P('dp')
- delta_grad: float32 [768, 24], P('dp', 'tensor')
- conv_inner_grad: float32 [4, 1536], P(None, 'tensor')
- shift_inner_grad: float32 [1536], P('tensor')
- conv_shared_grad: float32 [4, 256], replicated
- shift_shared_grad: float32 [256], replicated
- decay_log_grad: float32 [24], P('tensor')
- delta_bias_grad: float32 [24], P('tensor')
- bypass_factor_sensitivity: float32 [24], P('tensor')
- gated_gain_grad: float32 [1536], P('tensor')
- out_weight_grad: float32 [1536, 768], P('tensor', 'dp')
All inputs are finite; a program needn't handle non-finite values.
Results may differ from a plain program's by a relative error of at most 0.0095.
Values may be sent and summed in bfloat16 or wider, within the bound.
A program may use at most 320 MiB of HBM per device.

v0:
```python
import functools

import jax
import jax.numpy as jnp
from jax import lax
from jax.experimental import pallas as pl
from jax.experimental.pallas import tpu as pltpu
from jax.sharding import PartitionSpec as P

P_SIZE = 64
SPAN = 256
HALF = SPAN // 2
EPSILON = 1e-05
LOG2E = 1.4426950408889634
F32 = jnp.float32
BF16 = jnp.bfloat16
VMEM_LIMIT = 65024 * 1024
WIDE = 512


def dot(a, b):
    return jnp.dot(a, b, preferred_element_type=F32)


def dot_nt(a, b):
    return lax.dot_general(a, b, (((1,), (1,)), ((), ())), preferred_element_type=F32)


def dot_tn(a, b):
    return lax.dot_general(a, b, (((0,), (0,)), ((), ())), preferred_element_type=F32)


def sigmoid(v):
    return 0.5 * jnp.tanh(0.5 * v) + 0.5


def split2(v):
    hi = v.astype(BF16)
    return hi, (v - hi.astype(F32)).astype(BF16)


def lanes_of(shape):
    return lax.broadcasted_iota(jnp.int32, shape, len(shape) - 1)


def packed(v, heads):
    v = jnp.where(lanes_of(v.shape) < heads, v, 0.0)
    hi = v.astype(BF16).astype(F32)
    low = (v - hi).astype(BF16).astype(F32)
    return (hi + pltpu.roll(low, 32, 1)).astype(BF16)


def spread_heads(pk, sel):
    return dot(pk, sel)


def gather_heads(v, sel):
    hi, low = split2(v)
    return dot_nt(hi, sel) + dot_nt(low, sel)


def cumulate(tri, v, heads):
    v = jnp.where(lanes_of(v.shape) < heads, v, 0.0)
    p0 = v.astype(BF16).astype(F32)
    r = v - p0
    p1 = r.astype(BF16).astype(F32)
    p2 = r - p1
    pk = (p0 + pltpu.roll(p1, 32, 1) + pltpu.roll(p2, 64, 1)).astype(BF16)
    s = dot(tri, pk)
    n = s.shape[1]
    s = s + pltpu.roll(s, n - 32, 1) + pltpu.roll(s, n - 64, 1)
    return jnp.where(lanes_of(v.shape) < heads, s, 0.0)


def lane_tiles(v):
    return sum(v[:, c0 : c0 + 128] for c0 in range(0, v.shape[1], 128))


def row_tiles(v):
    return jnp.sum(v.reshape(v.shape[0] // 8, 8, v.shape[1]), axis=0)


def block_rows(b, size):
    return pl.ds(pl.multiple_of(b * size, size), size)


MESH = pl.DeviceIdType.MESH


class Sends:
    def __init__(self, send, recv):
        self.send, self.recv, self.used, self.started = send, recv, 0, []

    def make(self, src, dst, to):
        k = self.used
        self.used += 1
        return pltpu.make_async_remote_copy(
            src_ref=src, dst_ref=dst, send_sem=self.send.at[k], recv_sem=self.recv.at[k],
            device_id=to, device_id_type=MESH,
        )

    def start(self, src, dst, to):
        copy = self.make(src, dst, to)
        copy.start()
        self.started.append(copy)
        return copy

    def finish(self):
        for copy in self.started:
            copy.wait_send()


def hello(others):
    barrier = pltpu.get_barrier_semaphore()
    for to in others:
        pl.semaphore_signal(barrier, inc=1, device_id=to, device_id_type=MESH)


def greet(others):
    hello(others)
    pl.semaphore_wait(pltpu.get_barrier_semaphore(), len(others))


def place():
    z = lax.axis_index("tensor")
    d = lax.axis_index("dp")
    core = lax.rem(d, 2)
    x = lax.rem(d // 2, 2)
    y = d // 4
    return z, d, core, x, y


def xor_peer(core, x, y, k):
    c1 = 1 - core if k & 1 else core
    x1 = 1 - x if k & 2 else x
    y1 = 1 - y if k & 4 else y
    return y1 * 4 + x1 * 2 + c1


def dp_rows(d, size, part=None):
    if part is None:
        return pl.ds(pl.multiple_of(d * size, 16), size)
    return pl.ds(pl.multiple_of(d * size + part * (size // 2), 16), size // 2)


def columns(t, size):
    return pl.ds(pl.multiple_of(t * size, 128), size)


def cut_at(base, size, by_t, t):
    return pl.ds(pl.multiple_of(base + t * size, 128), size) if by_t else pl.ds(base, size)


class Gather:
    MESSAGES = 13

    def __init__(self, sends, nt, shard, full, here):
        self.sends, self.nt, self.shard, self.full = sends, nt, shard, full
        self.z, self.d, self.core, self.x, self.y = here
        self.rows, self.width = shard.shape

    def to(self, k):
        return {"dp": xor_peer(self.core, self.x, self.y, k)}

    def ref(self, k, part=None):
        return self.full.at[dp_rows(xor_peer(self.core, self.x, self.y, k), self.rows, part), :]

    def begin(self, sem):
        mine = self.full.at[dp_rows(self.d, self.rows), columns(self.z, self.width)]
        self.local = pltpu.make_async_copy(self.shard, mine, sem)
        self.local.start()
        self.zs = []
        for dz in range(1, self.nt):
            to = {"tensor": lax.rem(self.z + dz, self.nt)}
            self.zs.append(self.sends.start(self.shard, mine, to))

    def column(self):
        self.local.wait()
        for copy in self.zs:
            copy.wait_recv()
        own_a, own_b = self.ref(0, 0), self.ref(0, 1)
        self.x0 = self.sends.start(own_a, own_a, self.to(2))
        self.y0 = self.sends.start(own_b, own_b, self.to(4))
        self.c = [self.sends.start(self.ref(0), self.ref(0), self.to(1))]
        self.y1 = self.sends.start(own_a, own_a, self.to(4))
        self.x1 = self.sends.start(own_b, own_b, self.to(2))

    def forward(self):
        self.forward_first()
        self.forward_second()

    def forward_first(self):
        self.x0.wait_recv()
        self.y2 = self.sends.start(self.ref(2, 0), self.ref(2, 0), self.to(4))
        self.y0.wait_recv()
        self.x2 = self.sends.start(self.ref(4, 1), self.ref(4, 1), self.to(2))

    def forward_second(self):
        self.x1.wait_recv()
        self.c.append(self.sends.start(self.ref(2), self.ref(2), self.to(1)))
        self.y1.wait_recv()
        self.c.append(self.sends.start(self.ref(4), self.ref(4), self.to(1)))

    def corner(self):
        self.y2.wait_recv()
        self.x2.wait_recv()
        self.c.append(self.sends.start(self.ref(6), self.ref(6), self.to(1)))

    def finish(self):
        for copy in self.c:
            copy.wait_recv()


class Reduce:
    MESSAGES = 18

    @staticmethod
    def scratch(rows, width, nt, wz):
        half = rows // 2
        shapes = [(4, rows, width), (2, half, width), (2, half, width), (half, width), (half, width), (nt, rows, wz)]
        return [pltpu.VMEM(s, BF16) for s in shapes]

    def __init__(self, sends, nt, g, bufs, cuts, here):
        self.nt, self.g, self.cuts = nt, g, cuts
        self.rc, self.ra, self.rb, self.ta, self.tb, self.rz = bufs
        self.z, self.d, core, x, y = here
        rows = self.rc.shape[1]
        to = lambda k: {"dp": xor_peer(core, x, y, k)}
        at = lambda y, x, core, part=None: dp_rows(4 * y + 2 * x + core, rows, part)
        send = lambda src, dst, to: sends.make(g.at[src, :], dst, to)
        self.core = [send(at(q // 2, q % 2, 1 - core), self.rc.at[q], to(1)) for q in range(4)]
        self.core_rows = [at(q // 2, q % 2, core) for q in range(4)]
        self.a = [send(at(i, 1 - x, core, 0), self.ra.at[i], to(2)) for i in range(2)]
        self.b = [send(at(1 - y, i, core, 1), self.rb.at[i], to(4)) for i in range(2)]
        self.a_rows = [at(i, x, core, 0) for i in range(2)]
        self.b_rows = [at(y, i, core, 1) for i in range(2)]
        self.a2 = send(at(1 - y, x, core, 0), self.ta, to(4))
        self.b2 = send(at(y, 1 - x, core, 1), self.tb, to(2))
        self.halves = [dp_rows(self.d, rows, i) for i in range(2)]
        self.own = dp_rows(self.d, rows)
        self.zs = []
        self.places = []
        first = 0
        for base, size, by_t in cuts:
            dst = self.rz.at[self.z, :, pl.ds(first, size)]
            for dz in range(1, nt):
                t = lax.rem(self.z + dz, nt)
                src = g.at[self.own, cut_at(base, size, by_t, t)]
                self.zs.append(sends.make(src, dst, {"tensor": t}))
            self.places.append((first, size, cut_at(base, size, by_t, self.z)))
            first += size

    def add(self, rows, other):
        self.g[rows, :] = (self.g[rows, :].astype(F32) + other.astype(F32)).astype(BF16)

    def begin(self):
        for copy in self.core:
            copy.start()

    def first(self):
        for q in range(4):
            self.core[q].wait_recv()
            self.add(self.core_rows[q], self.rc[q])
        for copy in self.a + self.b:
            copy.start()

    def second(self):
        for i in range(2):
            self.a[i].wait_recv()
            self.add(self.a_rows[i], self.ra[i])
            self.b[i].wait_recv()
            self.add(self.b_rows[i], self.rb[i])
        self.a2.start()
        self.b2.start()

    def third(self):
        self.a2.wait_recv()
        self.add(self.halves[0], self.ta[...])
        self.b2.wait_recv()
        self.add(self.halves[1], self.tb[...])
        for copy in self.zs:
            copy.start()
        for first, size, cols in self.places:
            self.rz[self.z, :, first : first + size] = self.g[self.own, cols]

    def last(self, *outs):
        for copy in self.zs:
            copy.wait_recv()
        for out, (first, size, _) in zip(outs, self.places):
            total = self.rz[0, :, first : first + size].astype(F32)
            for t in range(1, self.nt):
                total = total + self.rz[t, :, first : first + size].astype(F32)
            out[...] = total

    def finish(self):
        for copy in self.core + self.a + self.b + [self.a2, self.b2] + self.zs:
            copy.wait_send()


class SmallSum:
    MESSAGES = 6

    @staticmethod
    def scratch(shape, nt):
        return [pltpu.VMEM((2,) + shape, F32), pltpu.VMEM((3,) + shape, F32), pltpu.VMEM((nt,) + shape, F32)]

    def __init__(self, sends, nt, v, bufs, here):
        self.nt, self.v = nt, v
        self.own, self.got, self.rz = bufs
        self.z, d, core, x, y = here
        self.copies = [
            sends.make(self.own.at[k - 1] if k else v, self.got.at[k], {"dp": xor_peer(core, x, y, 2**k)}) for k in range(3)
        ]
        part = self.rz.at[self.z]
        self.zs = [sends.make(part, part, {"tensor": lax.rem(self.z + dz, nt)}) for dz in range(1, nt)]

    def begin(self):
        self.copies[0].start()

    def step(self, k):
        self.copies[k - 1].wait_recv()
        total = (self.own[k - 2] if k > 1 else self.v[...]) + self.got[k - 1]
        if k < 3:
            self.own[k - 1] = total
            self.copies[k].start()
        else:
            self.rz[self.z] = total
            for copy in self.zs:
                copy.start()

    def finish(self):
        for copy in self.copies + self.zs:
            copy.wait_send()

    def last(self):
        for copy in self.zs:
            copy.wait_recv()
        total = self.rz[0]
        for t in range(1, self.nt):
            total = total + self.rz[t]
        return total


class Chain:
    def __init__(self, nt, by, mine, whole, got, out, send, recv):
        self.mine, self.whole, self.got, self.out, self.send, self.recv = mine, whole, got, out, send, recv
        z = lax.axis_index("tensor")
        self.seqs, _, di = got.shape
        self.per = di // WIDE
        self.pieces = self.seqs * self.per
        self.at = z if by > 0 else nt - 1 - z
        self.has_prev = self.at > 0
        self.has_next = self.at < nt - 1
        self.next = {"tensor": lax.rem(z + by + nt, nt)}
        self.begin_slot = 3 * self.at - 1

    def copy(self, k):
        s = k // self.per
        cols = pl.ds(pl.multiple_of((k - s * self.per) * WIDE, WIDE), WIDE)
        return pltpu.make_async_remote_copy(
            src_ref=self.out.at[s, :, cols], dst_ref=self.got.at[s, :, cols], send_sem=self.send.at[k],
            recv_sem=self.recv.at[k], device_id=self.next, device_id_type=MESH,
        )

    def pass_on(self, k, first):
        s = k // self.per
        cols = pl.ds(pl.multiple_of((k - s * self.per) * WIDE, WIDE), WIDE)
        v = self.mine[s, :, cols].astype(F32)
        if not first:
            v = v + self.whole[s, 0:1, cols] * self.got[s, :, cols].astype(F32)
        self.out[s, :, cols] = v.astype(BF16)
        self.copy(k).start()

    def begin(self, s):
        @pl.when(jnp.logical_not(self.has_prev))
        def _():
            self.got[s] = jnp.zeros(self.got.shape[1:], BF16)
            for k in range(self.per * s, self.per * (s + 1)):
                self.pass_on(k, True)

    def step(self, k):
        self.copy(k).wait_recv()

        @pl.when(self.has_next)
        def _():
            self.pass_on(k, False)

    def slot(self, n):
        since = n - self.begin_slot

        @pl.when(self.has_prev & self.has_next & (since >= 0) & (lax.rem(since + 8, 2) == 0) & (since < 2 * self.pieces))
        def _():
            self.step(since // 2)

    def rest(self, slots):
        for k in range(self.pieces):

            @pl.when(self.has_prev & self.has_next & (self.begin_slot + 2 * k >= slots))
            def _(k=k):
                self.step(k)

    def arrive(self, s):
        for i in range(self.per):

            @pl.when(jnp.logical_not(self.has_next))
            def _(i=i):
                self.copy(self.per * s + i).wait_recv()

    def finish(self):
        @pl.when(self.has_next)
        def _():
            for k in range(self.pieces):
                self.copy(k).wait_send()


class Moves:
    def __init__(self, sems):
        self.sems, self.used, self.open = sems, 0, []

    def start(self, src, dst):
        copy = pltpu.make_async_copy(src, dst, self.sems.at[self.used])
        self.used += 1
        copy.start()
        self.open.append(copy)
        return copy

    def finish(self, done=()):
        for copy in self.open:
            if all(copy is not other for other in done):
                copy.wait()


def heads_table(sel_ref, di):
    r = lax.broadcasted_iota(jnp.int32, (128, WIDE), 0)
    c = lax.broadcasted_iota(jnp.int32, (128, WIDE), 1)
    for c0 in range(0, di, WIDE):
        hit = ((r & 31) == ((c + c0) >> 6)) & (r < 64)
        sel_ref[:, c0 : c0 + WIDE] = jnp.where(hit, 1.0, 0.0).astype(BF16)


def ones_below(tri_ref, up):
    r = lax.broadcasted_iota(jnp.int32, (SPAN, SPAN), 0)
    c = lax.broadcasted_iota(jnp.int32, (SPAN, SPAN), 1)
    tri_ref[...] = jnp.where(r <= c if up else r >= c, 1.0, 0.0).astype(BF16)


def forward_kernel(heads, nt, nd, gathers, *refs):
    refs = list(refs)
    take = lambda n: [refs.pop(0) for _ in range(n)]
    x_hbm, c_hbm, norm_gain_ref, conv_shared_ref, shift_shared_ref = take(5)
    if gathers:
        (wgi_ref, wdelta_ref, wo_ref, wsh_ref, conv_inner_ref, shift_inner_ref, gated_gain_ref, decay_ref, bias_ref,
         skip_gain_ref) = take(10)
    else:
        w1_hbm, w2_hbm, w3_hbm, ws_hbm, parf_ref, xhf_ref = take(6)
    (h_hbm, rawi_hbm, raws_hbm, xs_hbm, bc_hbm, w1_out, w2_out, w3_out, ws_out, yn_hbm, dgate_hbm, dy_hbm, draw_hbm,
     acs_hbm, bs_hbm, rr_hbm, fresh_hbm, vv_hbm, mineb_hbm, sin_hbm) = take(20)
    (dec_ref, whole_ref, chan_ref, dpar_ref, skip_ref, gg_ref, sk_ref, ts_ref) = take(8)
    (x_ref, c_ref, h_ref, w1_ref, w2_ref, w3_ref, ws_ref, pf_ref, xh_ref, rawi_ref, raws_ref, xs_ref, bc_ref, y_ref,
     skc_ref, yn_ref, dgate_ref, dy_ref, g_ref, mine_ref, sb_ref, hh_ref, ea_ref, bst_ref,
     sel_ref, tri_ref, pack_ref, par_ref, zd_ref, wss_ref, turn_ref,
     draw_ref, acs_ref, bs_ref, rr_ref, fresh_ref, eaf_ref, vv_ref, mineb_ref, sin_ref, wk_ref) = take(41)
    send, recv, chain_send, chain_recv, local, moves, result_sems = take(7)

    tokens, dim = x_ref.shape
    seqs, ext, di = rawi_ref.shape
    span = ext - 16
    per = span // SPAN
    blocks = seqs * per
    sh = bc_ref.shape[1]
    state = sh // 2
    dcol = di // nt
    wa = dcol - 128
    inner = nt * wa
    z = lax.axis_index("tensor")
    store = Moves(moves)
    load_x = store.start(x_hbm, x_ref)
    load_c = store.start(c_hbm, c_ref)

    sends = Sends(send, recv)
    zpeers = [{"tensor": lax.rem(z + dz, nt)} for dz in range(1, nt)]
    if gathers:
        here = place()
        _, d, core, x, y = here
        others = zpeers + [{"dp": xor_peer(core, x, y, k)} for k in range(1, 8)]
        hello(others)
        rows = wgi_ref.shape[0]
        hloc = heads // nt
        pack_ref[:, :dcol] = wgi_ref[:, 1, :]
        pl.semaphore_wait(pltpu.get_barrier_semaphore(), len(others))
        shards = (
            (pack_ref.at[:, pl.ds(0, wa)], w1_ref.at[:, pl.ds(0, inner)]),
            (pack_ref.at[:, pl.ds(wa, 128)], w1_ref.at[:, pl.ds(inner, 128 * nt)]),
            (pack_ref.at[:, pl.ds(dcol, dcol)], w2_ref),
            (wo_ref, w3_ref),
        )
        secs = [Gather(sends, nt, a, b, here) for a, b in shards]
        secs[0].begin(local.at[0])
        secs[1].begin(local.at[1])
        pack_ref[:, dcol:] = wgi_ref[:, 0, :]
        turn_ref[...] = jnp.zeros_like(turn_ref)
        turn_ref[0:hloc, 0:rows] = wdelta_ref[...].astype(F32)
        zd_ref[z] = turn_ref[...].T[0:rows].astype(BF16)
        wss_ref[:, :sh] = wsh_ref[...]
        par_ref[...] = jnp.zeros_like(par_ref)
        par_ref[0:4, :] = conv_inner_ref[...].astype(F32)
        par_ref[4:5, :] = shift_inner_ref[...].astype(F32).reshape(1, dcol)
        par_ref[5:6, :] = gated_gain_ref[...].reshape(1, dcol)
        for k, ref in enumerate((decay_ref, bias_ref, skip_gain_ref)):
            par_ref[8 + k : 9 + k, 0:hloc] = ref[...].reshape(1, hloc)
        deltas = [sends.start(zd_ref.at[z], zd_ref.at[z], to) for to in zpeers]
        mine = ws_ref.at[dp_rows(d, rows), :]
        own = [pltpu.make_async_copy(wss_ref, mine, local.at[4]), pltpu.make_async_copy(par_ref, pf_ref.at[z], local.at[5])]
        own[1].start()
        got = [sends.start(par_ref, pf_ref.at[z], to) for to in zpeers]
        edges = [
            sends.make(
                x_hbm.at[pl.ds((s + 1) * span - 16, 16), :], xh_ref.at[pl.ds(16 * s, 16), :],
                {"tensor": lax.rem(z + 1, nt)},
            )
            for s in range(seqs)
        ]

        @pl.when(z < nt - 1)
        def _():
            for copy in edges:
                copy.start()

    else:
        greet(({"tensor": lax.rem(z + nt - 1, nt)}, {"tensor": lax.rem(z + 1, nt)}))
        loads = [store.start(a, b) for a, b in ((w1_hbm, w1_ref), (w2_hbm, w2_ref), (w3_hbm, w3_ref), (ws_hbm, ws_ref))]
        pf_ref[...] = parf_ref[...]
        xh_ref[...] = xhf_ref[...]

    heads_table(sel_ref, di)
    ones_below(tri_ref, False)

    gain = norm_gain_ref[...].reshape(1, dim)
    ts_ref[...] = jnp.zeros_like(ts_ref)
    ts_ref[0:4, :] = conv_shared_ref[...].astype(F32)
    ts_ref[4:5, :] = shift_shared_ref[...].astype(F32).reshape(1, sh)

    def norm(v):
        v = v.astype(F32)
        return (v * lax.rsqrt(jnp.mean(v * v, axis=-1, keepdims=True) + EPSILON) * gain).astype(BF16)

    load_x.wait()

    def norm_step(b, c):
        rows = block_rows(b, SPAN)
        h_ref[rows, :] = norm(x_ref[rows, :])
        return c

    lax.fori_loop(0, blocks, norm_step, 0)
    store.start(h_ref, h_hbm)

    if gathers:
        secs[0].column()
        for copy in deltas:
            copy.wait_recv()
        delta = zd_ref[0].astype(F32)
        for t in range(1, nt):
            delta = delta + pltpu.roll(zd_ref[t].astype(F32), hloc * t, 1)
        wss_ref[:, sh:] = delta.astype(BF16)
        own[0].start()
        got += [sends.start(wss_ref, mine, {"dp": xor_peer(core, x, y, k)}) for k in range(1, 8)]
        secs[1].column()
        secs[0].forward()
        secs[2].begin(local.at[2])
        secs[1].forward_first()

        @pl.when(z > 0)
        def _():
            for copy in edges:
                copy.wait_recv()

        @pl.when(z == 0)
        def _():
            xh_ref[...] = jnp.zeros_like(xh_ref)

        for copy in own:
            copy.wait()
        for copy in got:
            copy.wait_recv()

    hh_ref[...] = norm(xh_ref[...])
    head = pf_ref[0, 8:16, 0:128]
    for t in range(nt):
        chan_ref[:, dcol * t : dcol * (t + 1)] = pf_ref[t, 0:8, :]
        if t > 0:
            head = head + pltpu.roll(pf_ref[t, 8:16, 0:128], heads // nt * t, 1)
    ak = -jnp.exp(head[0:1])
    ak = jnp.where(lanes_of(ak.shape) < heads, ak, 0.0)
    dpar_ref[0:1, :] = head[1:2]
    dpar_ref[1:2, :] = ak * LOG2E
    dpar_ref[2:3, :] = ak
    dpar_ref[3:8, :] = jnp.zeros((5, 128), F32)
    sk8 = packed(jnp.broadcast_to(head[2:3], (8, 128)), heads)
    for c0 in range(0, di, WIDE):
        skip_ref[:, c0 : c0 + WIDE] = spread_heads(sk8, sel_ref[:, c0 : c0 + WIDE])

    def conv(raw, par, out, s, cols):
        def step(r, c):
            r0 = pl.multiple_of(r * 128, 128)
            v = raw[s, pl.ds(r0 + 8, 136), cols]
            acc = par[4:5, cols] + par[3:4, cols] * v[8:]
            for k in range(3):
                acc = acc + par[k : k + 1, cols] * v[5 + k : 133 + k]
            out[pl.ds(pl.multiple_of(s * span + r0, 128), 128), cols] = (acc * sigmoid(acc)).astype(BF16)
            return c

        lax.fori_loop(0, span // 128, step, 0)

    if not gathers:
        loads[3].wait()
    for s in range(seqs):
        rows = slice(span * s, span * (s + 1))
        raws_ref[s, 0:16, :] = dot(hh_ref[16 * s : 16 * s + 16, :], ws_ref[:, :sh])
        both = dot(h_ref[rows, :], ws_ref[...])
        raws_ref[s, 16:ext, :] = both[:, :sh]
        draw_ref[rows, :] = both[:, sh:] + dpar_ref[0:1, :]
        for c0 in range(0, sh, 256):
            conv(raws_ref, ts_ref, bc_ref, s, slice(c0, c0 + 256))
    store.start(raws_ref, raws_hbm)
    store.start(bc_ref, bc_hbm)
    store.start(ws_ref, ws_out)

    def first_part(s):
        def step(t, carry):
            cols = pl.ds(pl.multiple_of(dcol * t, 128), wa)
            w = w1_ref[:, pl.ds(pl.multiple_of(wa * t, 128), wa)]
            rawi_ref[s, 0:16, cols] = dot(hh_ref[16 * s : 16 * s + 16, :], w)
            rawi_ref[s, 16:ext, cols] = dot(h_ref[span * s : span * (s + 1), :], w)
            conv(rawi_ref, chan_ref, xs_ref, s, cols)
            return carry

        lax.fori_loop(0, nt, step, 0)

    def second_part(s):
        rows = slice(span * s, span * (s + 1))

        def step(t, carry):
            cols = pl.ds(pl.multiple_of(dcol * t + wa, 128), 128)
            w = w1_ref[:, pl.ds(pl.multiple_of(inner + 128 * t, 128), 128)]
            rawi_ref[s, 0:16, cols] = dot(hh_ref[16 * s : 16 * s + 16, :], w)
            rawi_ref[s, 16:ext, cols] = dot(h_ref[rows, :], w)
            conv(rawi_ref, chan_ref, xs_ref, s, cols)
            return carry

        lax.fori_loop(0, nt, step, 0)
        store.start(rawi_ref.at[s], rawi_hbm.at[s])
        store.start(xs_ref.at[rows, :], xs_hbm.at[rows, :])

    def block_step(s, j, c):
        b = s * per + j
        rows = block_rows(b, SPAN)
        bt = bc_ref[rows, :state].astype(F32).T.astype(BF16)
        w = spread_heads(wk_ref[rows, :], sel_ref[...])
        fresh = dot(bt, (w * xs_ref[rows, :].astype(F32)).astype(BF16))

        @pl.when(j == 0)
        def _():
            fresh_ref[s] = fresh.astype(BF16)
            mine_ref[s] = fresh

        @pl.when(j > 0)
        def _():
            mine_ref[s] = dec_ref[b, 0:1, :] * mine_ref[s] + fresh

        return c

    def decay_step(b, c):
        rows = block_rows(b, SPAN)
        s = b // per
        j = b - s * per
        x = draw_ref[rows, :]
        dt = jnp.maximum(x, 0.0) + jnp.log1p(jnp.exp(-jnp.abs(x)))
        lg = jnp.where(x < -20.0, x * LOG2E, jnp.log2(jnp.maximum(dt, 1e-30)))
        acs = cumulate(tri_ref[...], dt * dpar_ref[1:2, :], heads)
        bs = acs - lg
        acs_ref[rows, :] = acs
        bs_ref[rows, :] = bs
        bst_ref[b] = bs.T
        end = acs[SPAN - 1 : SPAN, :]
        wk_ref[rows, :] = packed(jnp.exp2(end - bs), heads)
        ea_ref[rows, :] = packed(jnp.exp2(acs), heads)
        de = spread_heads(packed(jnp.broadcast_to(jnp.exp2(end), (8, 128)), heads), sel_ref[...])
        dec_ref[b] = de

        @pl.when(j == 0)
        def _():
            whole_ref[s] = de

        @pl.when(j > 0)
        def _():
            whole_ref[s] = de * whole_ref[s]

        return c

    chain = Chain(nt, 1, mine_ref, whole_ref, sin_ref, sb_ref, chain_send, chain_recv)
    if gathers:
        secs[1].forward_second()
        secs[0].corner()
        secs[2].column()
        secs[3].begin(local.at[3])
        secs[1].corner()
    lax.fori_loop(0, blocks, decay_step, 0)
    for a, b in ((draw_ref, draw_hbm), (acs_ref, acs_hbm), (bs_ref, bs_hbm)):
        store.start(a, b)
    if gathers:
        secs[0].finish()
    else:
        loads[0].wait()
    for s in range(seqs):
        first_part(s)
        if gathers and s == 0:
            secs[2].forward_first()
    if gathers:
        secs[1].finish()
        secs[2].forward_second()
        secs[3].column()
    store.start(w1_ref, w1_out)
    for s in range(seqs):
        second_part(s)
        lax.fori_loop(0, per, functools.partial(block_step, s), 0)
        chain.begin(s)
        if s == seqs - 1:
            store.start(fresh_ref, fresh_hbm)
        if gathers and s == 0:
            secs[2].corner()
            secs[3].forward()
    if gathers:
        secs[3].corner()

    lower = lax.broadcasted_iota(jnp.int32, (HALF, HALF), 0) >= lax.broadcasted_iota(jnp.int32, (HALF, HALF), 1)
    first = lanes_of((HALF, 128)) < P_SIZE
    pairs = di // 128

    def intra_step(b, carry):
        rows = block_rows(b, SPAN)
        bb = bc_ref[rows, :state]
        cc = bc_ref[rows, state:]
        g00 = dot_nt(cc[:HALF], bb[:HALF])
        g10 = dot_nt(cc[HALF:], bb[:HALF])
        g11 = dot_nt(cc[HALF:], bb[HALF:])
        for p in range(pairs):
            cols = slice(128 * p, 128 * p + 128)
            xp = xs_ref[rows, cols]
            y0, y1 = [], []
            for h in (2 * p, 2 * p + 1):
                a0 = acs_ref[block_rows(2 * b, HALF), h : h + 1]
                a1 = acs_ref[block_rows(2 * b + 1, HALF), h : h + 1]
                r0 = bst_ref[b, h : h + 1, :HALF]
                r1 = bst_ref[b, h : h + 1, HALF:]
                m00 = jnp.where(lower, jnp.exp2(a0 - r0) * g00, 0.0).astype(BF16)
                m10 = (jnp.exp2(a1 - r0) * g10).astype(BF16)
                m11 = jnp.where(lower, jnp.exp2(a1 - r1) * g11, 0.0).astype(BF16)
                y0.append(dot(m00, xp[:HALF]))
                y1.append(dot(jnp.concatenate([m10, m11], axis=1), xp))
            y_ref[block_rows(2 * b, HALF), cols] = jnp.where(first, y0[0], y0[1])
            y_ref[block_rows(2 * b + 1, HALF), cols] = jnp.where(first, y1[0], y1[1])
            if (p + 1) % (pairs // 3) == 0:
                chain.slot(3 * b + (p + 1) // (pairs // 3) - 1)
        return carry

    lax.fori_loop(0, blocks, intra_step, 0)
    load_c.wait()
    if gathers:
        secs[2].finish()
    else:
        loads[1].wait()
        loads[2].wait()
    store.start(w2_ref, w2_out)

    def gate_step(b, carry):
        rows = block_rows(b, span)
        for c0 in range(0, di, WIDE):
            cols = slice(c0, c0 + WIDE)
            dy_ref[rows, cols] = dot(h_ref[rows, :], w2_ref[:, cols]).astype(BF16)
        return carry

    def products_step(b, carry):
        rows = block_rows(b, span)
        for c0 in range(0, di, WIDE):
            cols = slice(c0, c0 + WIDE)
            dgate_ref[rows, cols] = (dot(c_ref[rows, :], w3_ref[:, cols]) * chan_ref[5:6, cols]).astype(BF16)
        return carry

    lax.fori_loop(0, seqs, gate_step, 0)
    if gathers:
        secs[3].finish()
    store.start(w3_ref, w3_out)
    lax.fori_loop(0, seqs, products_step, 0)
    chain.rest(3 * blocks)

    gg_ref[...] = jnp.zeros_like(gg_ref)
    skc_ref[...] = jnp.zeros_like(skc_ref)
    results = ((yn_ref, yn_hbm), (dgate_ref, dgate_hbm), (dy_ref, dy_hbm), (rr_ref, rr_hbm))

    def result_copy(k, b):
        rows = block_rows(b, SPAN)
        return pltpu.make_async_copy(results[k][0].at[rows, :], results[k][1].at[rows, :], result_sems.at[k, b])

    def sin_copy(s):
        return pltpu.make_async_copy(sin_ref.at[s], sin_hbm.at[s], result_sems.at[len(results), s])

    def mid_step(s, j, carry):
        b = s * per + j
        rows = block_rows(b, SPAN)
        cc = bc_ref[rows, state:]
        ss = jnp.zeros((SPAN, 128), F32)
        for c0 in range(0, di, WIDE):
            cols = slice(c0, c0 + WIDE)
            prev = sin_ref[s, :, cols].astype(F32)
            later = dec_ref[s * per, 0:1, cols] * prev + fresh_ref[s, :, cols].astype(F32)
            s_in = jnp.where(j == 0, prev, later).astype(BF16)
            ea = spread_heads(ea_ref[rows, :], sel_ref[:, cols])
            eaf_ref[:, cols] = ea
            ynos = y_ref[rows, cols] + ea * dot(cc, s_in)
            y_ref[rows, cols] = ynos
            y = ynos + skip_ref[0:1, cols] * xs_ref[rows, cols].astype(F32)
            gate = dy_ref[rows, cols].astype(F32)
            g = y * (gate * sigmoid(gate))
            g_ref[:, cols] = g
            ss = ss + lane_tiles(g * g)
        r2 = lax.rsqrt(jnp.sum(ss, axis=-1, keepdims=True) / di + EPSILON)
        qg = jnp.zeros((SPAN, 128), F32)
        for c0 in range(0, di, WIDE):
            cols = slice(c0, c0 + WIDE)
            g = g_ref[:, cols]
            gain = chan_ref[5:6, cols]
            yn_ref[rows, cols] = (g * r2 * gain).astype(BF16)
            qg_here = dgate_ref[rows, cols].astype(F32) * g
            gg_ref[:, cols] += row_tiles(qg_here * r2)
            qg = qg + lane_tiles(qg_here)
        coef = r2 * r2 * r2 * (jnp.sum(qg, axis=-1, keepdims=True) / di)
        rr = jnp.zeros((SPAN, 128), F32)
        ct = cc.astype(F32).T.astype(BF16)
        for c0 in range(0, di, WIDE):
            cols = slice(c0, c0 + WIDE)
            xf = xs_ref[rows, cols].astype(F32)
            ynos = y_ref[rows, cols]
            y = ynos + skip_ref[0:1, cols] * xf
            gate = dy_ref[rows, cols].astype(F32)
            sg = sigmoid(gate)
            dg = r2 * dgate_ref[rows, cols].astype(F32) - coef * g_ref[:, cols]
            dgate_ref[rows, cols] = (dg * y * (sg * (1.0 + gate * (1.0 - sg)))).astype(BF16)
            dyb = (dg * (gate * sg)).astype(BF16)
            dy_ref[rows, cols] = dyb
            dy = dyb.astype(F32)
            rr = rr + gather_heads(dy * ynos, sel_ref[:, cols])
            skc_ref[:, cols] += row_tiles(dy * xf)
            vv = dot(ct, (eaf_ref[:, cols] * dy).astype(BF16))

            @pl.when(j == 0)
            def _(cols=cols, vv=vv):
                mine_ref[s, :, cols] = vv

            @pl.when(j > 0)
            def _(cols=cols, vv=vv):
                vv_ref[s, :, cols] = vv.astype(BF16)
                mine_ref[s, :, cols] += dec_ref[s * per, 0:1, cols] * vv

        rr_ref[rows, :] = rr
        for k in range(len(results)):
            result_copy(k, b).start()
        return carry

    def mid_sequence(s, carry):
        chain.arrive(s)
        sin_copy(s).start()
        lax.fori_loop(0, per, functools.partial(mid_step, s), 0)
        return carry

    lax.fori_loop(0, seqs, mid_sequence, 0)
    gg_ref[...] = gg_ref[...] / chan_ref[5:6, :]
    sk_ref[...] = jnp.zeros_like(sk_ref)
    for c0 in range(0, di, WIDE):
        sk_ref[...] += gather_heads(skc_ref[:, c0 : c0 + WIDE], sel_ref[:, c0 : c0 + WIDE])
    mineb_ref[...] = mine_ref[...].astype(BF16)
    chain.finish()
    sends.finish()
    if gathers:

        @pl.when(z < nt - 1)
        def _():
            for copy in edges:
                copy.wait_send()

    for s in range(seqs):
        sin_copy(s).wait()
    store.start(mineb_ref, mineb_hbm)
    store.start(vv_ref, vv_hbm)
    for b in range(blocks):
        for k in range(len(results)):
            result_copy(k, b).wait()
    store.finish((load_x, load_c) if gathers else (load_x, load_c, *loads))


def backward_kernel(heads, nt, nd, reduces, *refs):
    refs = list(refs)
    take = lambda n: [refs.pop(0) for _ in range(n)]
    (x_hbm, c_hbm, h_hbm, rawi_hbm, raws_hbm, xs_hbm, bc_hbm, w1_hbm, w2_hbm, w3_hbm, ws_hbm, yn_hbm, dgate_hbm, dy_hbm,
     draw_hbm, acs_hbm, bs_hbm, rr_hbm, fresh_hbm, vv_hbm, sin_hbm, mineb_hbm) = take(22)
    norm_gain_ref, ts_ref, dec_ref, whole_ref, chan_ref, dpar_ref, skip_ref, gg_ref, sk_ref = take(9)
    out_hbm, ig_hbm = take(2)
    if reduces:
        o1_ref, osd_ref, o2_ref, o3_ref, om_ref = take(5)
    else:
        g1_out, g2_out, g3_out, sm_ref = take(4)
    (c_ref, h_ref, rawi_ref, raws_ref, xs_ref, bc_ref, w1_ref, ws_ref, dgate_ref, dy_ref, draw_ref,
     acs_ref, bs_ref, rr_ref, fresh_ref, vv_ref, sin_ref, ds_ref, sb_ref, din_ref, dx_ref, dbc_ref, g_ref, halo_ref,
     edge_ref, keep_ref, acst_ref, dg_ref, sel_ref, triu_ref, tg_ref, small_ref, ng_ref, w2_ref) = take(34)
    if reduces:
        (sm_ref,) = take(1)
        bufs = [take(6) for _ in range(4)]
        small_bufs = take(3)
    chain_send, chain_recv, halo_send, halo_recv, moves = take(5)
    if reduces:
        sems = [take(2) for _ in range(5)]

    tokens, dim = h_ref.shape
    seqs, ext, di = rawi_ref.shape
    span = ext - 16
    per = span // SPAN
    blocks = seqs * per
    sh = bc_ref.shape[1]
    state = sh // 2
    dcol = di // nt
    wa = dcol - 128
    na = nt * wa
    z = lax.axis_index("tensor")
    move = Moves(moves)
    load = lambda a, b: move.start(a, b)
    yn_ref = din_ref.at[:, pl.ds(0, di)]
    l_mine, l_c, l_yn0 = load(mineb_hbm, sb_ref), load(c_hbm, c_ref), load(yn_hbm, yn_ref)
    x_ref = xs_ref.at[:, pl.ds(0, dim)]
    w3_ref = din_ref.at[pl.ds(0, dim), pl.ds(0, di)]

    if reduces:
        here = place()
        _, d, core, x, y = here
        others = [{"tensor": lax.rem(z + dz, nt)} for dz in range(1, nt)]
        others += [{"dp": xor_peer(core, x, y, k)} for k in (1, 2, 4)]
        hello(others)
        cut = ((0, dcol, True),)
        parts = (
            (g_ref.at[:, pl.ds(di, di)], cut), (g_ref.at[:, pl.ds(0, di)], cut),
            (g_ref.at[:, pl.ds(di, na)], ((0, wa, True),)),
            (g_ref.at[:, pl.ds(di + na, 128 * nt + sh + 128)], ((0, 128, True), (128 * nt, sh + 128, False))),
        )
        r3, r2, ra, rb = (Reduce(Sends(*sems[i]), nt, g, bufs[i], cuts, here) for i, (g, cuts) in enumerate(parts))
        small_sum = SmallSum(Sends(*sems[4]), nt, sm_ref, small_bufs, here)
    else:
        others = [{"tensor": lax.rem(z + nt - 1, nt)}, {"tensor": lax.rem(z + 1, nt)}]
        hello(others)
    heads_table(sel_ref, di)
    ones_below(triu_ref, True)
    small_ref[...] = jnp.zeros_like(small_ref)
    ng_ref[...] = jnp.zeros_like(ng_ref)
    tg_ref[...] = jnp.zeros_like(tg_ref)
    pl.semaphore_wait(pltpu.get_barrier_semaphore(), len(others))

    chain = Chain(nt, -1, sb_ref, whole_ref, ds_ref, sb_ref, chain_send, chain_recv)
    l_mine.wait()
    for s in range(seqs):
        chain.begin(s)

    def weight_gradient(dv, w, at):
        g = dot_tn(h_ref[...], dv)
        g_ref[:, at : at + g.shape[1]] = g.astype(BF16)
        ng_ref[...] += lane_tiles(g * w.astype(F32))

    l_c.wait()
    l_yn0.wait()
    l_h, l_dgate, l_w2 = load(h_hbm, h_ref), load(dgate_hbm, dgate_ref), load(w2_hbm, w2_ref)
    slot = 0
    for c0 in range(0, di, WIDE):
        g_ref[:, di + c0 : di + c0 + WIDE] = dot_tn(c_ref[...], din_ref[:, c0 : c0 + WIDE]).astype(BF16)
        chain.slot(slot)
        slot += 1
    if reduces:
        r3.begin()
    else:
        s3 = move.start(g_ref.at[:, pl.ds(di, di)], g3_out)
    l_h.wait()
    l_dgate.wait()
    l_w2.wait()
    l_scan = [
        load(a, b)
        for a, b in (
            (xs_hbm, xs_ref), (dy_hbm, dy_ref), (bc_hbm, bc_ref), (acs_hbm, acs_ref), (bs_hbm, bs_ref),
        )
    ]
    for c0 in range(0, di, WIDE):
        weight_gradient(dgate_ref[:, c0 : c0 + WIDE], w2_ref[:, c0 : c0 + WIDE], c0)
        chain.slot(slot)
        slot += 1
    if reduces:
        r2.begin()
    else:
        s2 = move.start(g_ref.at[:, pl.ds(0, di)], g2_out)

    for copy in l_scan:
        copy.wait()
    l_state = [
        load(a, b)
        for a, b in (
            (draw_hbm, draw_ref), (rr_hbm, rr_ref), (fresh_hbm, fresh_ref), (vv_hbm, vv_ref), (sin_hbm, sin_ref),
            (rawi_hbm, rawi_ref), (raws_hbm, raws_ref),
        )
    ]
    l_last = [load(w1_hbm, w1_ref), load(ws_hbm, ws_ref)]
    upper = lax.broadcasted_iota(jnp.int32, (HALF, HALF), 0) <= lax.broadcasted_iota(jnp.int32, (HALF, HALF), 1)
    first = lanes_of((HALF, 128)) < P_SIZE
    first_all = lanes_of((SPAN, 128)) < P_SIZE
    pairs = di // 128
    slot0 = slot

    def intra_step(b, carry):
        rows = block_rows(b, SPAN)
        acst_ref[...] = acs_ref[rows, :].T
        bb = bc_ref[rows, :state]
        cc = bc_ref[rows, state:]
        g00 = dot_nt(bb[:HALF], cc[:HALF])
        g01 = dot_nt(bb[:HALF], cc[HALF:])
        g11 = dot_nt(bb[HALF:], cc[HALF:])
        dg_ref[...] = jnp.zeros_like(dg_ref)
        for p in range(pairs):
            cols = slice(128 * p, 128 * p + 128)
            xp = xs_ref[rows, cols]
            dyp = dy_ref[rows, cols]
            d0, d1 = [], []
            for i, h in enumerate((2 * p, 2 * p + 1)):
                keep = first_all if i == 0 else jnp.logical_not(first_all)
                xm = jnp.where(keep, xp, jnp.zeros_like(xp))
                b0 = bs_ref[block_rows(2 * b, HALF), h : h + 1]
                b1 = bs_ref[block_rows(2 * b + 1, HALF), h : h + 1]
                r0 = acst_ref[h : h + 1, :HALF]
                r1 = acst_ref[h : h + 1, HALF:]
                e00 = jnp.where(upper, jnp.exp2(r0 - b0), 0.0)
                e01 = jnp.exp2(r1 - b0)
                e11 = jnp.where(upper, jnp.exp2(r1 - b1), 0.0)
                m0 = jnp.concatenate([(e00 * g00).astype(BF16), (e01 * g01).astype(BF16)], axis=1)
                m1 = (e11 * g11).astype(BF16)
                d0.append(dot(m0, dyp))
                d1.append(dot(m1, dyp[HALF:]))
                dm0 = dot_nt(xm[:HALF], dyp)
                dm1 = dot_nt(xm[HALF:], dyp[HALF:])
                dg_ref[0] += dm0[:, :HALF] * e00
                dg_ref[1] += dm0[:, HALF:] * e01
                dg_ref[2] += dm1 * e11
            dx_ref[block_rows(2 * b, HALF), cols] = jnp.where(first, d0[0], d0[1])
            dx_ref[block_rows(2 * b + 1, HALF), cols] = jnp.where(first, d1[0], d1[1])
            if reduces and p == pairs // 2:
                pl.when(b == blocks // 4)(r3.first)
            if (p + 1) % (pairs // 3) == 0:
                chain.slot(slot0 + 3 * b + (p + 1) // (pairs // 3) - 1)
        dg00 = dg_ref[0]
        dg01 = dg_ref[1]
        dg11 = dg_ref[2]
        dbc_ref[block_rows(2 * b, HALF), :state] = dot(jnp.concatenate([dg00, dg01], axis=1).astype(BF16), cc)
        dbc_ref[block_rows(2 * b + 1, HALF), :state] = dot(dg11.astype(BF16), cc[HALF:])
        dbc_ref[block_rows(2 * b, HALF), state:] = dot(dg00.T.astype(BF16), bb[:HALF])
        dbc_ref[block_rows(2 * b + 1, HALF), state:] = dot(
            jnp.concatenate([dg01.T, dg11.T], axis=1).astype(BF16), bb
        )
        return carry

    lax.fori_loop(0, blocks, intra_step, 0)
    if reduces:
        r3.second()
        r2.first()
    chain.rest(slot0 + 3 * blocks)
    for copy in l_state:
        copy.wait()

    def state_step(s, j):
        b = s * per + j
        rows = block_rows(b, SPAN)
        acs = acs_ref[rows, :]
        end = acs[SPAN - 1 : SPAN, :]
        eak = packed(jnp.exp2(acs), heads)
        wk = packed(jnp.exp2(end - bs_ref[rows, :]), heads)
        bb = bc_ref[rows, :state]
        db = dbc_ref[rows, :state]
        dc = dbc_ref[rows, state:]
        pp = jnp.zeros((SPAN, 128), F32)
        endsum = jnp.zeros((8, 128), F32)
        for c0 in range(0, di, WIDE):
            cols = slice(c0, c0 + WIDE)
            s_in = sin_ref[s, :, cols]
            ds = ds_ref[s, :, cols]
            if j > 0:
                s_in = dec_ref[s * per, 0:1, cols] * s_in.astype(F32) + fresh_ref[s, :, cols].astype(F32)
                s_in = s_in.astype(BF16)
            if j < per - 1:
                ds = dec_ref[s * per + per - 1, 0:1, cols] * ds.astype(F32) + vv_ref[s, :, cols].astype(F32)
                ds = ds.astype(BF16)
            w = spread_heads(wk, sel_ref[:, cols])
            ea = spread_heads(eak, sel_ref[:, cols])
            xf = xs_ref[rows, cols].astype(F32)
            dyf = dy_ref[rows, cols].astype(F32)
            dxs = w * dot(bb, ds)
            dxn = dx_ref[rows, cols] + dxs
            pp = pp + gather_heads(dxn * xf, sel_ref[:, cols])
            at_end = jnp.sum(ds.astype(F32) * s_in.astype(F32), axis=0, keepdims=True) * dec_ref[b, 0:1, cols]
            first_row = lax.broadcasted_iota(jnp.int32, (8, WIDE), 0) == 0
            at_end = row_tiles(dxs * xf) + jnp.where(first_row, jnp.broadcast_to(at_end, (8, WIDE)), 0.0)
            endsum = endsum + gather_heads(at_end, sel_ref[:, cols])
            dc = dc + dot_nt((ea * dyf).astype(BF16), s_in)
            db = db + dot_nt((w * xf).astype(BF16), ds)
            dx_ref[rows, cols] = dxn + skip_ref[0:1, cols] * dyf
        dbc_ref[rows, :state] = db
        dbc_ref[rows, state:] = dc
        da = cumulate(triu_ref[...], rr_ref[rows, :] - pp, heads)
        da = da + jnp.sum(endsum, axis=0, keepdims=True)
        xx = draw_ref[rows, :]
        sg = 1.0 / (1.0 + jnp.exp(-xx))
        dt = jnp.maximum(xx, 0.0) + jnp.log1p(jnp.exp(-jnp.abs(xx)))
        ratio = jnp.where(xx < -20.0, 1.0, sg / jnp.maximum(dt, 1e-30))
        ak = dpar_ref[2:3, :]
        dd = da * ak * sg + pp * ratio
        din_ref[rows, di + sh :] = dd.astype(BF16)
        small_ref[0:1, :] += jnp.sum(da * dt * ak, axis=0, keepdims=True)
        small_ref[1:2, :] += jnp.sum(dd, axis=0, keepdims=True)

        def conv_back(raw, par, dact, off, cols):
            here_cols = pl.ds(pl.multiple_of(off + cols.start, 128), cols.size)

            def step(r, prev):
                r0 = pl.multiple_of(r * HALF, HALF)
                at = pl.ds(pl.multiple_of(16 + j * SPAN + r0, 16), HALF)
                now = raw[s, at, cols]
                v = jnp.concatenate([prev, now], axis=0)
                sh_v = [v[5 + k : 5 + k + HALF] for k in range(3)] + [now]
                pre = par[4:5, cols] + par[0:1, cols] * sh_v[0]
                for k in range(1, 4):
                    pre = pre + par[k : k + 1, cols] * sh_v[k]
                sg = sigmoid(pre)
                dp = dact[pl.ds(pl.multiple_of(b * SPAN + r0, HALF), HALF), cols] * (sg * (1.0 + pre * (1.0 - sg)))
                raw[s, at, cols] = dp
                for k in range(4):
                    tg_ref[k, :, here_cols] += row_tiles(dp * sh_v[k])
                tg_ref[4, :, here_cols] += row_tiles(dp)
                return now[HALF - 8 :]

            prev = raw[s, 8:16, cols] if j == 0 else keep_ref[s, :, here_cols]
            prev = lax.fori_loop(0, SPAN // HALF, step, prev)
            if j < per - 1:
                keep_ref[s, :, here_cols] = prev

        def inner_step(i, carry):
            conv_back(rawi_ref, chan_ref, dx_ref, 0, pl.ds(pl.multiple_of(256 * i, 256), 256))
            return carry

        lax.fori_loop(0, di // 256, inner_step, 0)
        for c0 in range(0, sh, 256):
            conv_back(raws_ref, ts_ref, dbc_ref, di, pl.ds(c0, 256))

    halo_copy = pltpu.make_async_remote_copy(
        src_ref=edge_ref, dst_ref=halo_ref, send_sem=halo_send.at[0], recv_sem=halo_recv.at[0],
        device_id={"tensor": lax.rem(z + nt - 1, nt)}, device_id_type=MESH,
    )
    for j in range(per):

        def seq_step(s, carry, j=j):
            if j == 0:
                chain.arrive(s)
            state_step(s, j)
            return carry

        lax.fori_loop(0, seqs, seq_step, 0)
        if j == 0:
            edge_ref[:, :, :di] = rawi_ref[:, 16:24, :]
            edge_ref[:, :, di:] = raws_ref[:, 16:24, :]

            @pl.when(z > 0)
            def _():
                halo_copy.start()

            if reduces:
                r3.third()
    l_last += [load(x_hbm, x_ref)]
    l_yn = load(yn_hbm, dy_ref)
    if reduces:
        r3.last(o3_ref)
        r2.second()

    @pl.when(z < nt - 1)
    def _():
        halo_copy.wait_recv()

    @pl.when(z == nt - 1)
    def _():
        halo_ref[...] = jnp.zeros_like(halo_ref)

    def conv_t(dpre, par, off, c0, to):
        cols = pl.ds(pl.multiple_of(c0, 128), 128)
        halo_cols = pl.ds(pl.multiple_of(off + c0, 128), 128)
        to_cols = pl.ds(pl.multiple_of(to, 128), 128)

        def step(s, carry):
            def rows_step(r, nxt):
                r0 = pl.multiple_of(span - HALF * (r + 1), HALF)
                now = dpre[s, pl.ds(pl.multiple_of(16 + r0, 16), HALF), cols]
                v = jnp.concatenate([now, nxt], axis=0)
                acc = par[3:4, cols] * now
                for k in range(3):
                    acc = acc + par[k : k + 1, cols] * v[3 - k : 3 - k + HALF]
                din_ref[pl.ds(pl.multiple_of(s * span + r0, HALF), HALF), to_cols] = acc.astype(BF16)
                return now[0:8]

            lax.fori_loop(0, span // HALF, rows_step, halo_ref[s, :, halo_cols])
            return carry

        lax.fori_loop(0, seqs, step, 0)

    def inner_first(i, carry):
        t = i // (wa // 128)
        r = 128 * (i - t * (wa // 128))
        conv_t(rawi_ref, chan_ref, 0, dcol * t + r, wa * t + r)
        return carry

    def inner_second(t, carry):
        conv_t(rawi_ref, chan_ref, 0, dcol * t + wa, na + 128 * t)
        return carry

    def shared_part(i, carry):
        conv_t(raws_ref, ts_ref, di, 128 * i, di + 128 * i)
        return carry

    lax.fori_loop(0, na // 128, inner_first, 0)
    if reduces:
        r3.finish()
        r2.third()
    else:
        s3.wait()
    for copy in l_last:
        copy.wait()
    for c0 in range(0, na, WIDE):
        weight_gradient(din_ref[:, c0 : c0 + WIDE], w1_ref[:, c0 : c0 + WIDE], di + c0)
    if reduces:
        ra.begin()
    lax.fori_loop(0, nt, inner_second, 0)
    lax.fori_loop(0, sh // 128, shared_part, 0)
    for c0 in range(na, di, WIDE):
        weight_gradient(din_ref[:, c0 : c0 + WIDE], w1_ref[:, c0 : c0 + WIDE], di + c0)
    weight_gradient(din_ref[:, di:], ws_ref[...], 2 * di)
    column = lambda v: jnp.sum(v, axis=0, keepdims=True)
    for k in range(5):
        sm_ref[k : k + 1, :] = column(tg_ref[k, :, :di])
    sm_ref[5:6, :] = column(gg_ref[...])
    gain = norm_gain_ref[...].reshape(1, dim)
    sm_ref[6:7, :dim] = column(ng_ref[...].T) / gain
    flat = [column(tg_ref[k, :, di:]) for k in range(5)] + [small_ref[0:1, :], small_ref[1:2, :], column(sk_ref[...])]
    row, at = 6, dim
    for v in flat:
        width = v.shape[1]
        if at + width > di:
            row, at = row + 1, 0
        sm_ref[row : row + 1, at : at + width] = v
        at += width
    sm_ref[row : row + 1, at:] = jnp.zeros((1, di - at), F32)
    if reduces:
        rb.begin()
        small_sum.begin()
    else:
        move.start(g_ref.at[:, pl.ds(di, g_ref.shape[1] - di)], g1_out)
    def last_step(b, carry):
        if reduces:
            pl.when(b == 0)(ra.first)

            @pl.when(b == blocks // 4)
            def _():
                small_sum.step(1)
                rb.first()

            @pl.when(b == 2 * blocks // 4)
            def _():
                small_sum.step(2)

            @pl.when(b == 3 * blocks // 4)
            def _():
                ra.second()
                small_sum.step(3)

        rows = block_rows(b, SPAN)
        dh = dot_nt(dgate_ref[rows, :], w2_ref[...])
        dh = dh + dot_nt(din_ref[rows, :di], w1_ref[...])
        dh = dh + dot_nt(din_ref[rows, di:], ws_ref[...])
        u = x_ref[rows, :].astype(F32)
        r1 = lax.rsqrt(jnp.mean(u * u, axis=-1, keepdims=True) + EPSILON)
        e = dh * gain
        m = jnp.mean(e * u, axis=-1, keepdims=True)
        c_ref[rows, :] = (c_ref[rows, :].astype(F32) + r1 * e - u * (r1 * r1 * r1 * m)).astype(BF16)
        return carry

    lax.fori_loop(0, blocks, last_step, 0)
    move.start(c_ref, ig_hbm)
    l_w3 = load(w3_hbm, w3_ref)

    def output_step(b, carry):
        rows = block_rows(b, SPAN)
        x_ref[rows, :] = (x_ref[rows, :].astype(F32) + dot_nt(dy_ref[rows, :], w3_ref[...])).astype(BF16)
        return carry

    if reduces:
        rb.second()
        ra.third()
    l_w3.wait()
    l_yn.wait()
    lax.fori_loop(0, blocks // 2, output_step, 0)
    if reduces:
        rb.third()
    lax.fori_loop(blocks // 2, blocks, output_step, 0)
    move.start(x_ref, out_hbm)
    if reduces:
        r2.last(o2_ref)
        om_ref[...] = small_sum.last()
        ra.last(o1_ref.at[:, pl.ds(0, wa)])
        rb.last(o1_ref.at[:, pl.ds(wa, 128)], osd_ref)
        for part in (r2, ra, rb, small_sum):
            part.finish()
    chain.finish()

    @pl.when(z > 0)
    def _():
        halo_copy.wait_send()

    move.finish((l_mine, l_c, l_yn0, l_yn, l_w3, l_h, l_dgate, l_w2, *l_scan, *l_state, *l_last) + (() if reduces else (s3,)))


def finish_kernel(nt, hloc, out_hbm, ig_hbm, o1_ref, osd_ref, o2_ref, o3_ref, om_ref, *refs):
    (out_to, ig_to, ng_ref, gi_ref, gs_ref, delta_ref, ci_ref, si_ref, cs_ref, ss_ref, decay_ref, bias_ref, bypass_ref,
     gg_ref, ow_ref, out_ref, ig_ref, sems) = refs
    ways = ((out_hbm, out_ref, out_to), (ig_hbm, ig_ref, ig_to))
    into = [pltpu.make_async_copy(a, b, sems.at[k]) for k, (a, b, _) in enumerate(ways)]
    onto = [pltpu.make_async_copy(b, c, sems.at[2 + k]) for k, (_, b, c) in enumerate(ways)]
    for copy in into:
        copy.start()
    z = lax.axis_index("tensor")
    dcol = o1_ref.shape[1]
    sh = gs_ref.shape[1]
    dim = ng_ref.shape[0]
    cols = pl.ds(pl.multiple_of(z * dcol, 128), dcol)
    back = lax.rem(128 - z * hloc, 128)
    ng_ref[...] = om_ref[6, :dim]
    gi_ref[:, 0, :] = o2_ref[...]
    gi_ref[:, 1, :] = o1_ref[...]
    gs_ref[...] = osd_ref[:, :sh]
    delta_ref[...] = pltpu.roll(osd_ref[:, sh:], back, 1).T[:hloc]
    ci_ref[...] = om_ref[0:4, cols]
    si_ref[...] = om_ref[4, cols]
    gg_ref[...] = om_ref[5, cols]
    row, at = 6, dim
    taps = []
    for _ in range(5):
        if at + sh > om_ref.shape[1]:
            row, at = row + 1, 0
        taps.append(om_ref[row : row + 1, at : at + sh])
        at += sh
    for k in range(4):
        cs_ref[k : k + 1, :] = taps[k]
    ss_ref[...] = taps[4][0]
    for ref in (decay_ref, bias_ref, bypass_ref):
        if at + 128 > om_ref.shape[1]:
            row, at = row + 1, 0
        v = jnp.broadcast_to(om_ref[row : row + 1, at : at + 128], (8, 128))
        ref[...] = pltpu.roll(v, back, 1)[0, :hloc]
        at += 128
    for copy, after in zip(into, onto):
        copy.wait()
        after.start()
    ow_ref[...] = o3_ref[...]
    for copy in onto:
        copy.wait()


def semaphores(n):
    return [pltpu.SemaphoreType.DMA((n,)), pltpu.SemaphoreType.DMA((n,))]


def shifted(v, axis, by):
    n = lax.axis_size(axis)
    return lax.ppermute(v, axis, [(i, i + by) for i in range(n) if 0 <= i + by < n])


def gather_all(nt, nd, wgi, wdelta, wo, ws, par, edge):
    both = ("tensor", "dp")
    rows = ws.shape[0]
    dcol = wo.shape[0]
    pack = jnp.concatenate([wgi[:, 1], wgi[:, 0], wo.T], axis=1)
    full = lax.all_gather(pack, both, axis=0).reshape(nt, nd * rows, -1)
    whole = lambda a, b: full[:, :, a:b].transpose(1, 0, 2).reshape(nd * rows, nt * (b - a))
    w1 = jnp.concatenate([whole(0, dcol - 128), whole(dcol - 128, dcol)], axis=1)
    delta = lax.all_gather(wdelta, "tensor", axis=1, tiled=True)
    delta = jnp.pad(delta, ((0, 0), (0, 128 - delta.shape[1])))
    return (
        w1, whole(dcol, 2 * dcol), whole(2 * dcol, 3 * dcol),
        lax.all_gather(jnp.concatenate([ws, delta], axis=1), "dp", axis=0, tiled=True),
        lax.all_gather(par, "tensor", axis=0), shifted(edge, "tensor", 1),
    )


def reduce_all(nt, nd, g1, g2, g3, sm, sh):
    dim = g1.shape[0]
    rows = dim // nd
    dcol = g2.shape[1] // nt
    wa = dcol - 128
    both = ("tensor", "dp")
    parts = [
        g[:, at : at + nt * w].reshape(dim, nt, w).transpose(1, 0, 2)
        for g, at, w in ((g1, 0, wa), (g1, wa * nt, 128), (g2, 0, dcol), (g3, 0, dcol))
    ]
    big = jnp.concatenate(parts, axis=2).reshape(nt * nd, rows, -1)
    big = lax.psum_scatter(big, both, scatter_dimension=0).astype(F32)
    shared = g1[:, nt * dcol :].reshape(nd, rows, sh + 128).astype(F32)
    shared = lax.psum(lax.psum_scatter(shared, "dp", scatter_dimension=0), "tensor")
    return big[:, :dcol], shared, big[:, dcol : 2 * dcol], big[:, 2 * dcol :], lax.psum(sm, both)


def local(
    block_input, norm_gain, input_gate_inner_weight, input_shared_weight, input_delta_weight, conv_inner, shift_inner,
    conv_shared, shift_shared, decay_log, delta_bias, skip_gain, gated_gain, output_projection_weight, cotangent,
):
    nt = lax.axis_size("tensor")
    nd = lax.axis_size("dp")
    me = lax.axis_index("tensor")
    seqs, span, dim = block_input.shape
    tokens = seqs * span
    blocks = tokens // SPAN
    rows, _, dcol = input_gate_inner_weight.shape
    di = dcol * nt
    sh = input_shared_weight.shape[1]
    state = sh // 2
    hloc = input_delta_weight.shape[1]
    heads = hloc * nt

    x = block_input.reshape(tokens, dim)
    c = cotangent.reshape(tokens, dim)
    gathers = nd == 8
    args = [x, c, norm_gain, conv_shared, shift_shared]
    kinds = [pl.ANY, pl.ANY] + [pltpu.VMEM] * 3
    if gathers:
        args += [
            input_gate_inner_weight, input_delta_weight.T, output_projection_weight.T, input_shared_weight, conv_inner,
            shift_inner, gated_gain, decay_log, delta_bias, skip_gain,
        ]
        kinds += [pltpu.VMEM] * 10
    else:
        head = jnp.pad(jnp.stack([decay_log, delta_bias, skip_gain]), ((0, 5), (0, dcol - hloc)))
        par = [conv_inner.astype(F32), shift_inner.astype(F32)[None], gated_gain[None], jnp.zeros((2, dcol), F32), head]
        args += gather_all(
            nt, nd, input_gate_inner_weight, input_delta_weight, output_projection_weight, input_shared_weight,
            jnp.concatenate(par, axis=0), block_input[:, span - 16 :].reshape(seqs * 16, dim),
        )
        kinds += [pl.ANY] * 4 + [pltpu.VMEM] * 2
    scan_state = ((seqs, state, di), BF16)
    f128 = ((tokens, 128), F32)
    far = [
        ((tokens, dim), BF16), ((seqs, span + 16, di), F32), ((seqs, span + 16, sh), F32), ((tokens, di), BF16),
        ((tokens, sh), BF16), ((dim, di), BF16), ((dim, di), BF16), ((dim, di), BF16), ((dim, sh + 128), BF16),
        ((tokens, di), BF16), ((tokens, di), BF16), ((tokens, di), BF16), f128, f128, f128, f128, scan_state,
        scan_state, scan_state, scan_state,
    ]
    near = [
        ((blocks, 8, di), F32), ((seqs, 8, di), F32), ((8, di), F32), ((8, 128), F32), ((8, di), F32), ((8, di), F32),
        ((8, 128), F32), ((8, sh), F32)]
    scratch = [
        ((tokens, dim), BF16), ((tokens, dim), BF16), ((tokens, dim), BF16), ((dim, di), BF16), ((dim, di), BF16),
        ((dim, di), BF16), ((dim, sh + 128), BF16), ((nt, 16, dcol), F32), ((seqs * 16, dim), BF16),
        ((seqs, span + 16, di), F32), ((seqs, span + 16, sh), F32), ((tokens, di), BF16), ((tokens, sh), BF16),
        ((tokens, di), F32), ((8, di), F32), ((tokens, di), BF16), ((tokens, di), BF16), ((tokens, di), BF16),
        ((SPAN, di), F32), ((seqs, state, di), F32), scan_state,
        ((seqs * 16, dim), BF16), ((tokens, 128), BF16), ((blocks, 128, SPAN), F32), ((128, di), BF16),
        ((SPAN, SPAN), BF16), ((rows, 2 * dcol), BF16), ((16, dcol), F32), ((nt, rows, 128), BF16), ((rows, sh + 128), BF16),
        ((128, 128), F32), f128, f128, f128, f128, scan_state, ((SPAN, di), F32), scan_state, scan_state, scan_state,
        ((tokens, 128), BF16),
    ]
    pieces = seqs * di // WIDE
    h, rawi, raws, xs, bc, w1, w2, w3, ws, yn, dgate, dy, draw, acs, bs, rr, fresh, vv, mineb, sin, *rest = pl.pallas_call(
        functools.partial(forward_kernel, heads, nt, nd, gathers),
        out_shape=[jax.ShapeDtypeStruct(s, d) for s, d in far + near],
        in_specs=[pl.BlockSpec(memory_space=k) for k in kinds],
        out_specs=[pl.BlockSpec(memory_space=pl.ANY)] * len(far) + [pl.BlockSpec(memory_space=pltpu.VMEM)] * len(near),
        scratch_shapes=[pltpu.VMEM(s, d) for s, d in scratch]
        + semaphores(4 * Gather.MESSAGES + 5 + 2 * nt + seqs) + semaphores(pieces)
        + [pltpu.SemaphoreType.DMA((6,)), pltpu.SemaphoreType.DMA((24,)), pltpu.SemaphoreType.DMA((5, blocks))],
        compiler_params=pltpu.CompilerParams(vmem_limit_bytes=VMEM_LIMIT, collective_id=0, has_side_effects=True),
        name="forward",
    )(*args)
    dec, whole, chan, dpar, skip, ggg, skg, ts = rest

    args = [x, c, h, rawi, raws, xs, bc, w1, w2, w3, ws, yn, dgate, dy, draw, acs, bs, rr, fresh, vv, sin, mineb]
    kinds = [pl.ANY] * len(args)
    more = [norm_gain, ts, dec, whole, chan, dpar, skip, ggg, skg]
    args += more
    kinds += [pltpu.VMEM] * len(more)
    wa = dcol - 128
    scratch = [
        ((tokens, dim), BF16), ((tokens, dim), BF16), ((seqs, span + 16, di), F32),
        ((seqs, span + 16, sh), F32), ((tokens, di), BF16), ((tokens, sh), BF16), ((dim, di), BF16),
        ((dim, sh + 128), BF16), ((tokens, di), BF16), ((tokens, di), BF16), f128, f128, f128, f128, scan_state, scan_state,
        scan_state, scan_state, scan_state, ((tokens, di + sh + 128), BF16), ((tokens, di), F32), ((tokens, sh), F32),
        ((dim, 2 * di + sh + 128), BF16), ((seqs, 8, di + sh), F32), ((seqs, 8, di + sh), F32), ((seqs, 8, di + sh), F32),
        ((128, SPAN), F32), ((3, HALF, HALF), F32), ((128, di), BF16), ((SPAN, SPAN), BF16),
        ((5, 8, di + sh), F32), ((8, 128), F32), ((dim, 128), F32), ((dim, di), BF16),
    ]
    scratch = [pltpu.VMEM(s, d) for s, d in scratch]
    sems = semaphores(pieces) + semaphores(1) + [pltpu.SemaphoreType.DMA((32,))]
    if gathers:
        near = [
            ((rows, dcol), F32), ((rows, sh + 128), F32), ((rows, dcol), F32), ((rows, dcol), F32), ((8, di), F32)
        ]
        far = []
        scratch += [pltpu.VMEM((8, di), F32)]
        for width, wz in ((di, dcol), (di, dcol), (wa * nt, wa), (128 * nt + sh + 128, sh + 256)):
            scratch += Reduce.scratch(rows, width, nt, wz)
        scratch += SmallSum.scratch((8, di), nt)
        for _ in range(4):
            sems += semaphores(Reduce.MESSAGES)
        sems += semaphores(SmallSum.MESSAGES)
    else:
        far = [((dim, di + sh + 128), BF16), ((dim, di), BF16), ((dim, di), BF16)]
        near = [((8, di), F32)]
    outs = [((tokens, dim), BF16)] * 2 + far + near
    out, ig, *rest = pl.pallas_call(
        functools.partial(backward_kernel, heads, nt, nd, gathers),
        out_shape=[jax.ShapeDtypeStruct(s, d) for s, d in outs],
        in_specs=[pl.BlockSpec(memory_space=k) for k in kinds],
        out_specs=[pl.BlockSpec(memory_space=pl.ANY)] * (2 + len(far)) + [pl.BlockSpec(memory_space=pltpu.VMEM)] * len(near),
        scratch_shapes=scratch + sems,
        compiler_params=pltpu.CompilerParams(vmem_limit_bytes=VMEM_LIMIT, collective_id=1, has_side_effects=True),
        name="backward",
    )(*args)
    if gathers:
        sums = rest
    else:
        sums = reduce_all(nt, nd, *rest, sh)
    finals = [
        ((tokens, dim), BF16), ((tokens, dim), BF16), ((dim,), F32), ((rows, 2, dcol), F32), ((rows, sh), F32),
        ((hloc, rows), F32), ((4, dcol), F32), ((dcol,), F32), ((4, sh), F32), ((sh,), F32), ((hloc,), F32), ((hloc,), F32),
        ((hloc,), F32), ((dcol,), F32), ((rows, dcol), F32),
    ]
    out, ig, *rest = pl.pallas_call(
        functools.partial(finish_kernel, nt, hloc),
        out_shape=[jax.ShapeDtypeStruct(s, d) for s, d in finals],
        in_specs=[pl.BlockSpec(memory_space=pl.ANY)] * 2 + [pl.BlockSpec(memory_space=pltpu.VMEM)] * 5,
        out_specs=[pl.BlockSpec(memory_space=pl.ANY)] * 2 + [pl.BlockSpec(memory_space=pltpu.VMEM)] * 13,
        scratch_shapes=[pltpu.VMEM((tokens, dim), BF16)] * 2 + [pltpu.SemaphoreType.DMA((4,))],
        name="finish",
    )(out, ig, *sums)
    rest[3] = rest[3].T
    rest[-1] = rest[-1].T
    return (out.reshape(block_input.shape), ig.reshape(block_input.shape), *rest)


def solution(mesh):
    placed = (
        P("dp", "tensor", None), P(), P("dp", None, "tensor"), P("dp", None), P("dp", "tensor"), P(None, "tensor"),
        P("tensor"), P(), P(), P("tensor"), P("tensor"), P("tensor"), P("tensor"), P("tensor", "dp"),
        P("dp", "tensor", None),
    )
    return jax.shard_map(
        local,
        mesh=mesh,
        in_specs=placed,
        out_specs=(
            P("dp", "tensor", None), P("dp", "tensor", None), P(), P("dp", None, "tensor"), P("dp", None),
            P("dp", "tensor"), P(None, "tensor"), P("tensor"), P(), P(), P("tensor"), P("tensor"), P("tensor"),
            P("tensor"), P("tensor", "dp"),
        ),
        check_vma=False,
    )
```

profile of v0, /device:TPU:0, one launch (start us, length us, event | category | flops | bytes accessed | tf_op | source)
XLA Modules:
  0.0 184.0 jit_solution(2844996471841297350)
XLA Ops:
  0.7 84.3 %forward.1 = (bf16[1024,768]{1,0:T(8,128)(2,1)}, f32[2,528,1536]{2,1,0:T(8,128)}, f32[2,528,256]{2,1,0:T(8,128)}, bf16[1024,1536]{1,0:T(8,128)(2,1)}, bf16[1024,...) custom-call(bf16[1024,768]{1,0:T(8,128)(2,1)} %bitcast.8, ...), custom_call_target="tpu_custom_call" | custom-call | tf_op jit(solution)/shard_map/forward/pallas_call | solution.py:1482
  84.9 93.8 %backward.1 = (bf16[1024,768]{1,0:T(8,128)(2,1)}, bf16[1024,768]{1,0:T(8,128)(2,1)}, f32[96,384]{1,0:T(8,128)}, f32[96,384]{1,0:T(8,128)}, f32[96,384]{1,0:T(8,1...) custom-call(bf16[1024,768]{1,0:T(8,128)(2,1)} %bitcast.9, bf16[1024,768]{1,0:T(8,128)(2,1)} %bitcast.11, ...), custom_call_target="tpu_custom_call" | custom-call | tf_op jit(solution)/shard_map/backward/pallas_call | solution.py:1528
  178.7 5.1 %finish.1 = (bf16[1024,768]{1,0:T(8,128)(2,1)}, bf16[1024,768]{1,0:T(8,128)(2,1)}, f32[768]{0:T(1024)}, f32[96,2,384]{2,1,0:T(2,128)}, f32[96,256]{1,0:T(8,128)}...) custom-call(bf16[1024,768]{1,0:T(8,128)(2,1)} %get-tuple-element.93., ...), custom_call_target="tpu_custom_call" | custom-call | tf_op jit(solution)/shard_map/finish/pallas_call | solution.py:1546
where the time goes:
time: 185 us; the launch traced here: 184 us
  Pallas kernels  183 us (99%)
    pallas_call x1, Pallas kernels, local(): pl.pallas_call(functools.partial(backward_kernel, heads, nt, nd, gathers)...  93.8 us
    pallas_call x1, Pallas kernels, local(): pl.pallas_call(functools.partial(forward_kernel, heads, nt, nd, gathers),...  84.3 us
    pallas_call x1, Pallas kernels, local(): pl.pallas_call(functools.partial(finish_kernel, nt, hloc), out_shape=[jax...  5.11 us

commit v1 on v0

--- a/solution.py
+++ b/solution.py
@@ -16,6 +16,7 @@
 BF16 = jnp.bfloat16
 VMEM_LIMIT = 65024 * 1024
 WIDE = 512
+PIECES = 512, 256
 
 
 def dot(a, b):
@@ -342,21 +343,23 @@
 
 
 class Chain:
-    def __init__(self, nt, by, mine, whole, got, out, send, recv):
+    def __init__(self, nt, by, mine, whole, got, out, send, recv, piece, slots, near, far):
         self.mine, self.whole, self.got, self.out, self.send, self.recv = mine, whole, got, out, send, recv
         z = lax.axis_index("tensor")
         self.seqs, _, di = got.shape
-        self.per = di // WIDE
+        self.piece = piece
+        self.per = di // piece
         self.pieces = self.seqs * self.per
         self.at = z if by > 0 else nt - 1 - z
         self.has_prev = self.at > 0
         self.has_next = self.at < nt - 1
         self.next = {"tensor": lax.rem(z + by + nt, nt)}
-        self.begin_slot = 3 * self.at - 1
+        self.slots = slots
+        self.when = [jnp.where(self.at == 1, a, b) for a, b in zip(near, far)]
 
     def copy(self, k):
         s = k // self.per
-        cols = pl.ds(pl.multiple_of((k - s * self.per) * WIDE, WIDE), WIDE)
+        cols = pl.ds(pl.multiple_of((k - s * self.per) * self.piece, self.piece), self.piece)
         return pltpu.make_async_remote_copy(
             src_ref=self.out.at[s, :, cols], dst_ref=self.got.at[s, :, cols], send_sem=self.send.at[k],
             recv_sem=self.recv.at[k], device_id=self.next, device_id_type=MESH,
@@ -364,7 +367,7 @@
 
     def pass_on(self, k, first):
         s = k // self.per
-        cols = pl.ds(pl.multiple_of((k - s * self.per) * WIDE, WIDE), WIDE)
+        cols = pl.ds(pl.multiple_of((k - s * self.per) * self.piece, self.piece), self.piece)
         v = self.mine[s, :, cols].astype(F32)
         if not first:
             v = v + self.whole[s, 0:1, cols] * self.got[s, :, cols].astype(F32)
@@ -386,16 +389,19 @@
             self.pass_on(k, False)
 
     def slot(self, n):
-        since = n - self.begin_slot
-
-        @pl.when(self.has_prev & self.has_next & (since >= 0) & (lax.rem(since + 8, 2) == 0) & (since < 2 * self.pieces))
+        k, hit = 0, 0
+        for at in self.when:
+            k = k + jnp.where(at < n, 1, 0)
+            hit = hit + jnp.where(at == n, 1, 0)
+
+        @pl.when(self.has_prev & self.has_next & (hit == 1))
         def _():
-            self.step(since // 2)
-
-    def rest(self, slots):
-        for k in range(self.pieces):
-
-            @pl.when(self.has_prev & self.has_next & (self.begin_slot + 2 * k >= slots))
+            self.step(k)
+
+    def rest(self, first, last, now=True):
+        for k in range(first, last):
+
+            @pl.when(self.has_prev & self.has_next & (self.when[k] >= self.slots) & now)
             def _(k=k):
                 self.step(k)
 
@@ -495,8 +501,8 @@
             (wo_ref, w3_ref),
         )
         secs = [Gather(sends, nt, a, b, here) for a, b in shards]
+        secs[1].begin(local.at[1])
         secs[0].begin(local.at[0])
-        secs[1].begin(local.at[1])
         pack_ref[:, dcol:] = wgi_ref[:, 0, :]
         turn_ref[...] = jnp.zeros_like(turn_ref)
         turn_ref[0:hloc, 0:rows] = wdelta_ref[...].astype(F32)
@@ -555,7 +561,7 @@
     store.start(h_ref, h_hbm)
 
     if gathers:
-        secs[0].column()
+        secs[1].column()
         for copy in deltas:
             copy.wait_recv()
         delta = zd_ref[0].astype(F32)
@@ -564,10 +570,10 @@
         wss_ref[:, sh:] = delta.astype(BF16)
         own[0].start()
         got += [sends.start(wss_ref, mine, {"dp": xor_peer(core, x, y, k)}) for k in range(1, 8)]
-        secs[1].column()
-        secs[0].forward()
+        secs[0].column()
+        secs[1].forward()
         secs[2].begin(local.at[2])
-        secs[1].forward_first()
+        secs[0].forward_first()
 
         @pl.when(z > 0)
         def _():
@@ -648,8 +654,6 @@
             return carry
 
         lax.fori_loop(0, nt, step, 0)
-        store.start(rawi_ref.at[s], rawi_hbm.at[s])
-        store.start(xs_ref.at[rows, :], xs_hbm.at[rows, :])
 
     def block_step(s, j, c):
         b = s * per + j
@@ -697,40 +701,43 @@
 
         return c
 
-    chain = Chain(nt, 1, mine_ref, whole_ref, sin_ref, sb_ref, chain_send, chain_recv)
+    chain = Chain(
+        nt, 1, mine_ref, whole_ref, sin_ref, sb_ref, chain_send, chain_recv, PIECES[0],
+        3 * blocks + 2 * seqs, (2, 7, 12, 13, 14, 15), (10, 12, 14, 16, 17, 18),
+    )
     if gathers:
-        secs[1].forward_second()
-        secs[0].corner()
-        secs[2].column()
-        secs[3].begin(local.at[3])
         secs[1].corner()
+        secs[0].forward_second()
     lax.fori_loop(0, blocks, decay_step, 0)
     for a, b in ((draw_ref, draw_hbm), (acs_ref, acs_hbm), (bs_ref, bs_hbm)):
         store.start(a, b)
     if gathers:
-        secs[0].finish()
+        secs[1].finish()
+        secs[0].corner()
+        secs[2].column()
+        secs[3].begin(local.at[3])
     else:
         loads[0].wait()
     for s in range(seqs):
-        first_part(s)
-        if gathers and s == 0:
-            secs[2].forward_first()
+        second_part(s)
     if gathers:
-        secs[1].finish()
-        secs[2].forward_second()
-        secs[3].column()
+        secs[0].finish()
+        secs[2].forward_first()
     store.start(w1_ref, w1_out)
     for s in range(seqs):
-        second_part(s)
+        first_part(s)
+        store.start(rawi_ref.at[s], rawi_hbm.at[s])
+        store.start(xs_ref.at[pl.ds(span * s, span), :], xs_hbm.at[pl.ds(span * s, span), :])
         lax.fori_loop(0, per, functools.partial(block_step, s), 0)
         chain.begin(s)
         if s == seqs - 1:
             store.start(fresh_ref, fresh_hbm)
         if gathers and s == 0:
+            secs[2].forward_second()
+            secs[3].column()
             secs[2].corner()
-            secs[3].forward()
     if gathers:
-        secs[3].corner()
+        secs[3].forward()
 
     lower = lax.broadcasted_iota(jnp.int32, (HALF, HALF), 0) >= lax.broadcasted_iota(jnp.int32, (HALF, HALF), 1)
     first = lanes_of((HALF, 128)) < P_SIZE
@@ -755,10 +762,12 @@
                 m00 = jnp.where(lower, jnp.exp2(a0 - r0) * g00, 0.0).astype(BF16)
                 m10 = (jnp.exp2(a1 - r0) * g10).astype(BF16)
                 m11 = jnp.where(lower, jnp.exp2(a1 - r1) * g11, 0.0).astype(BF16)
-                y0.append(dot(m00, xp[:HALF]))
-                y1.append(dot(jnp.concatenate([m10, m11], axis=1), xp))
-            y_ref[block_rows(2 * b, HALF), cols] = jnp.where(first, y0[0], y0[1])
-            y_ref[block_rows(2 * b + 1, HALF), cols] = jnp.where(first, y1[0], y1[1])
+                y0.append(m00)
+                y1.append(jnp.concatenate([m10, m11], axis=1))
+            y0 = dot(jnp.concatenate(y0, axis=0), xp[:HALF])
+            y1 = dot(jnp.concatenate(y1, axis=0), xp)
+            y_ref[block_rows(2 * b, HALF), cols] = jnp.where(first, y0[:HALF], y0[HALF:])
+            y_ref[block_rows(2 * b + 1, HALF), cols] = jnp.where(first, y1[:HALF], y1[HALF:])
             if (p + 1) % (pairs // 3) == 0:
                 chain.slot(3 * b + (p + 1) // (pairs // 3) - 1)
         return carry
@@ -766,6 +775,7 @@
     lax.fori_loop(0, blocks, intra_step, 0)
     load_c.wait()
     if gathers:
+        secs[3].corner()
         secs[2].finish()
     else:
         loads[1].wait()
@@ -774,16 +784,26 @@
 
     def gate_step(b, carry):
         rows = block_rows(b, span)
-        for c0 in range(0, di, WIDE):
-            cols = slice(c0, c0 + WIDE)
+
+        def column_step(i, c):
+            cols = columns(i, WIDE)
             dy_ref[rows, cols] = dot(h_ref[rows, :], w2_ref[:, cols]).astype(BF16)
+            return c
+
+        lax.fori_loop(0, di // WIDE, column_step, 0)
+        chain.slot(3 * blocks + b)
         return carry
 
     def products_step(b, carry):
         rows = block_rows(b, span)
-        for c0 in range(0, di, WIDE):
-            cols = slice(c0, c0 + WIDE)
+
+        def column_step(i, c):
+            cols = columns(i, WIDE)
             dgate_ref[rows, cols] = (dot(c_ref[rows, :], w3_ref[:, cols]) * chan_ref[5:6, cols]).astype(BF16)
+            return c
+
+        lax.fori_loop(0, di // WIDE, column_step, 0)
+        chain.slot(3 * blocks + seqs + b)
         return carry
 
     lax.fori_loop(0, seqs, gate_step, 0)
@@ -791,7 +811,7 @@
         secs[3].finish()
     store.start(w3_ref, w3_out)
     lax.fori_loop(0, seqs, products_step, 0)
-    chain.rest(3 * blocks)
+    chain.rest(0, chain.per)
 
     gg_ref[...] = jnp.zeros_like(gg_ref)
     skc_ref[...] = jnp.zeros_like(skc_ref)
@@ -864,6 +884,8 @@
         rr_ref[rows, :] = rr
         for k in range(len(results)):
             result_copy(k, b).start()
+        chain.rest(chain.per, chain.pieces - 1, (s == 0) & (j == 0))
+        chain.rest(chain.pieces - 1, chain.pieces, (s == 0) & (j == per - 1))
         return carry
 
     def mid_sequence(s, carry):
@@ -961,24 +983,30 @@
     tg_ref[...] = jnp.zeros_like(tg_ref)
     pl.semaphore_wait(pltpu.get_barrier_semaphore(), len(others))
 
-    chain = Chain(nt, -1, sb_ref, whole_ref, ds_ref, sb_ref, chain_send, chain_recv)
+    chain = Chain(
+        nt, -1, sb_ref, whole_ref, ds_ref, sb_ref, chain_send, chain_recv, PIECES[1], 2 * (di // WIDE) + 3 * blocks,
+        (1, 2, 3, 4, 5, 6, 7, 8, 9, 10, 11, 12), (4, 5, 6, 7, 8, 9, 10, 11, 12, 13, 14, 15),
+    )
     l_mine.wait()
     for s in range(seqs):
         chain.begin(s)
 
     def weight_gradient(dv, w, at):
         g = dot_tn(h_ref[...], dv)
-        g_ref[:, at : at + g.shape[1]] = g.astype(BF16)
+        g_ref[:, pl.ds(pl.multiple_of(at, 128), g.shape[1])] = g.astype(BF16)
         ng_ref[...] += lane_tiles(g * w.astype(F32))
 
     l_c.wait()
     l_yn0.wait()
     l_h, l_dgate, l_w2 = load(h_hbm, h_ref), load(dgate_hbm, dgate_ref), load(w2_hbm, w2_ref)
-    slot = 0
-    for c0 in range(0, di, WIDE):
-        g_ref[:, di + c0 : di + c0 + WIDE] = dot_tn(c_ref[...], din_ref[:, c0 : c0 + WIDE]).astype(BF16)
-        chain.slot(slot)
-        slot += 1
+    parts = di // WIDE
+
+    def output_gradient(i, carry):
+        g_ref[:, columns(parts + i, WIDE)] = dot_tn(c_ref[...], din_ref[:, columns(i, WIDE)]).astype(BF16)
+        chain.slot(i)
+        return carry
+
+    lax.fori_loop(0, parts, output_gradient, 0)
     if reduces:
         r3.begin()
     else:
@@ -992,10 +1020,15 @@
             (xs_hbm, xs_ref), (dy_hbm, dy_ref), (bc_hbm, bc_ref), (acs_hbm, acs_ref), (bs_hbm, bs_ref),
         )
     ]
-    for c0 in range(0, di, WIDE):
-        weight_gradient(dgate_ref[:, c0 : c0 + WIDE], w2_ref[:, c0 : c0 + WIDE], c0)
-        chain.slot(slot)
-        slot += 1
+
+    def gate_gradient(i, carry):
+        cols = columns(i, WIDE)
+        weight_gradient(dgate_ref[:, cols], w2_ref[:, cols], i * WIDE)
+        chain.slot(parts + i)
+        return carry
+
+    lax.fori_loop(0, parts, gate_gradient, 0)
+    slot0 = 2 * parts
     if reduces:
         r2.begin()
     else:
@@ -1015,7 +1048,6 @@
     first = lanes_of((HALF, 128)) < P_SIZE
     first_all = lanes_of((SPAN, 128)) < P_SIZE
     pairs = di // 128
-    slot0 = slot
 
     def intra_step(b, carry):
         rows = block_rows(b, SPAN)
@@ -1030,10 +1062,12 @@
             cols = slice(128 * p, 128 * p + 128)
             xp = xs_ref[rows, cols]
             dyp = dy_ref[rows, cols]
-            d0, d1 = [], []
-            for i, h in enumerate((2 * p, 2 * p + 1)):
-                keep = first_all if i == 0 else jnp.logical_not(first_all)
-                xm = jnp.where(keep, xp, jnp.zeros_like(xp))
+            zero = jnp.zeros_like(xp)
+            xa, xb = jnp.where(first_all, xp, zero), jnp.where(first_all, zero, xp)
+            dm0 = dot_nt(jnp.concatenate([xa[:HALF], xb[:HALF]], axis=0), dyp)
+            dm1 = dot_nt(jnp.concatenate([xa[HALF:], xb[HALF:]], axis=0), dyp[HALF:])
+            d0, d1, de = [], [], []
+            for h in (2 * p, 2 * p + 1):
                 b0 = bs_ref[block_rows(2 * b, HALF), h : h + 1]
                 b1 = bs_ref[block_rows(2 * b + 1, HALF), h : h + 1]
                 r0 = acst_ref[h : h + 1, :HALF]
@@ -1043,15 +1077,16 @@
                 e11 = jnp.where(upper, jnp.exp2(r1 - b1), 0.0)
                 m0 = jnp.concatenate([(e00 * g00).astype(BF16), (e01 * g01).astype(BF16)], axis=1)
                 m1 = (e11 * g11).astype(BF16)
-                d0.append(dot(m0, dyp))
-                d1.append(dot(m1, dyp[HALF:]))
-                dm0 = dot_nt(xm[:HALF], dyp)
-                dm1 = dot_nt(xm[HALF:], dyp[HALF:])
-                dg_ref[0] += dm0[:, :HALF] * e00
-                dg_ref[1] += dm0[:, HALF:] * e01
-                dg_ref[2] += dm1 * e11
-            dx_ref[block_rows(2 * b, HALF), cols] = jnp.where(first, d0[0], d0[1])
-            dx_ref[block_rows(2 * b + 1, HALF), cols] = jnp.where(first, d1[0], d1[1])
+                d0.append(m0)
+                d1.append(m1)
+                de.append((e00, e01, e11))
+            d0 = dot(jnp.concatenate(d0, axis=0), dyp)
+            d1 = dot(jnp.concatenate(d1, axis=0), dyp[HALF:])
+            dg_ref[0] += dm0[:HALF, :HALF] * de[0][0] + dm0[HALF:, :HALF] * de[1][0]
+            dg_ref[1] += dm0[:HALF, HALF:] * de[0][1] + dm0[HALF:, HALF:] * de[1][1]
+            dg_ref[2] += dm1[:HALF] * de[0][2] + dm1[HALF:] * de[1][2]
+            dx_ref[block_rows(2 * b, HALF), cols] = jnp.where(first, d0[:HALF], d0[HALF:])
+            dx_ref[block_rows(2 * b + 1, HALF), cols] = jnp.where(first, d1[:HALF], d1[HALF:])
             if reduces and p == pairs // 2:
                 pl.when(b == blocks // 4)(r3.first)
             if (p + 1) % (pairs // 3) == 0:
@@ -1071,7 +1106,7 @@
     if reduces:
         r3.second()
         r2.first()
-    chain.rest(slot0 + 3 * blocks)
+    chain.rest(0, chain.per + 1)
     for copy in l_state:
         copy.wait()
 
@@ -1166,6 +1201,7 @@
 
         def seq_step(s, carry, j=j):
             if j == 0:
+                chain.rest(chain.per + 1, chain.pieces, s == 1)
                 chain.arrive(s)
             state_step(s, j)
             return carry
@@ -1238,14 +1274,18 @@
         s3.wait()
     for copy in l_last:
         copy.wait()
-    for c0 in range(0, na, WIDE):
-        weight_gradient(din_ref[:, c0 : c0 + WIDE], w1_ref[:, c0 : c0 + WIDE], di + c0)
+
+    def inner_gradient(i, carry):
+        cols = columns(i, WIDE)
+        weight_gradient(din_ref[:, cols], w1_ref[:, cols], di + i * WIDE)
+        return carry
+
+    lax.fori_loop(0, na // WIDE, inner_gradient, 0)
     if reduces:
         ra.begin()
     lax.fori_loop(0, nt, inner_second, 0)
     lax.fori_loop(0, sh // 128, shared_part, 0)
-    for c0 in range(na, di, WIDE):
-        weight_gradient(din_ref[:, c0 : c0 + WIDE], w1_ref[:, c0 : c0 + WIDE], di + c0)
+    lax.fori_loop(na // WIDE, di // WIDE, inner_gradient, 0)
     weight_gradient(din_ref[:, di:], ws_ref[...], 2 * di)
     column = lambda v: jnp.sum(v, axis=0, keepdims=True)
     for k in range(5):
@@ -1478,7 +1518,7 @@
         ((128, 128), F32), f128, f128, f128, f128, scan_state, ((SPAN, di), F32), scan_state, scan_state, scan_state,
         ((tokens, 128), BF16),
     ]
-    pieces = seqs * di // WIDE
+    pieces = seqs * di // min(PIECES)
     h, rawi, raws, xs, bc, w1, w2, w3, ws, yn, dgate, dy, draw, acs, bs, rr, fresh, vv, mineb, sin, *rest = pl.pallas_call(
         functools.partial(forward_kernel, heads, nt, nd, gathers),
         out_shape=[jax.ShapeDtypeStruct(s, d) for s, d in far + near],

time: 185 us -> 182 us (0.984)
  Pallas kernels: 183 us -> 181 us
    pallas_call x1, Pallas kernels: 93.8 us -> 91.2 us  [local(): pl.pallas_call(functools.partial(backward_kernel, heads, nt, nd, gathers)...]
where the time goes in v1:
time: 182 us
  Pallas kernels  181 us (99%)
    pallas_call x1, Pallas kernels, local(): pl.pallas_call(functools.partial(backward_kernel, heads, nt, nd, gathers)...  91.2 us
    pallas_call x1, Pallas kernels, local(): pl.pallas_call(functools.partial(forward_kernel, heads, nt, nd, gathers),...  84.8 us
    pallas_call x1, Pallas kernels, local(): pl.pallas_call(functools.partial(finish_kernel, nt, hloc), out_shape=[jax...  5.11 us

profile of v1, /device:TPU:0, one launch (start us, length us, event | category | flops | bytes accessed | tf_op | source)
XLA Modules:
  0.0 181.9 jit_solution(11598566608523190034)
XLA Ops:
  0.7 84.8 %forward.1 = (bf16[1024,768]{1,0:T(8,128)(2,1)}, f32[2,528,1536]{2,1,0:T(8,128)}, f32[2,528,256]{2,1,0:T(8,128)}, bf16[1024,1536]{1,0:T(8,128)(2,1)}, bf16[1024,...) custom-call(bf16[1024,768]{1,0:T(8,128)(2,1)} %bitcast.8, ...), custom_call_target="tpu_custom_call" | custom-call | tf_op jit(solution)/shard_map/forward/pallas_call | solution.py:1522
  85.4 91.2 %backward.1 = (bf16[1024,768]{1,0:T(8,128)(2,1)}, bf16[1024,768]{1,0:T(8,128)(2,1)}, f32[96,384]{1,0:T(8,128)}, f32[96,384]{1,0:T(8,128)}, f32[96,384]{1,0:T(8,1...) custom-call(bf16[1024,768]{1,0:T(8,128)(2,1)} %bitcast.9, bf16[1024,768]{1,0:T(8,128)(2,1)} %bitcast.11, ...), custom_call_target="tpu_custom_call" | custom-call | tf_op jit(solution)/shard_map/backward/pallas_call | solution.py:1568
  176.6 5.1 %finish.1 = (bf16[1024,768]{1,0:T(8,128)(2,1)}, bf16[1024,768]{1,0:T(8,128)(2,1)}, f32[768]{0:T(1024)}, f32[96,2,384]{2,1,0:T(2,128)}, f32[96,256]{1,0:T(8,128)}...) custom-call(bf16[1024,768]{1,0:T(8,128)(2,1)} %get-tuple-element.93., ...), custom_call_target="tpu_custom_call" | custom-call | tf_op jit(solution)/shard_map/finish/pallas_call | solution.py:1586

commit v2 on v1

--- a/solution.py
+++ b/solution.py
@@ -1374,9 +1374,14 @@
 def finish_kernel(nt, hloc, out_hbm, ig_hbm, o1_ref, osd_ref, o2_ref, o3_ref, om_ref, *refs):
     (out_to, ig_to, ng_ref, gi_ref, gs_ref, delta_ref, ci_ref, si_ref, cs_ref, ss_ref, decay_ref, bias_ref, bypass_ref,
      gg_ref, ow_ref, out_ref, ig_ref, sems) = refs
-    ways = ((out_hbm, out_ref, out_to), (ig_hbm, ig_ref, ig_to))
+    half = out_ref.shape[0] // 2
+    ways = [
+        tuple(ref.at[pl.ds(half * i, half), :] for ref in way)
+        for i in range(2)
+        for way in ((out_hbm, out_ref, out_to), (ig_hbm, ig_ref, ig_to))
+    ]
     into = [pltpu.make_async_copy(a, b, sems.at[k]) for k, (a, b, _) in enumerate(ways)]
-    onto = [pltpu.make_async_copy(b, c, sems.at[2 + k]) for k, (_, b, c) in enumerate(ways)]
+    onto = [pltpu.make_async_copy(b, c, sems.at[4 + k]) for k, (_, b, c) in enumerate(ways)]
     for copy in into:
         copy.start()
     z = lax.axis_index("tensor")
@@ -1588,7 +1593,7 @@
         out_shape=[jax.ShapeDtypeStruct(s, d) for s, d in finals],
         in_specs=[pl.BlockSpec(memory_space=pl.ANY)] * 2 + [pl.BlockSpec(memory_space=pltpu.VMEM)] * 5,
         out_specs=[pl.BlockSpec(memory_space=pl.ANY)] * 2 + [pl.BlockSpec(memory_space=pltpu.VMEM)] * 13,
-        scratch_shapes=[pltpu.VMEM((tokens, dim), BF16)] * 2 + [pltpu.SemaphoreType.DMA((4,))],
+        scratch_shapes=[pltpu.VMEM((tokens, dim), BF16)] * 2 + [pltpu.SemaphoreType.DMA((8,))],
         name="finish",
     )(out, ig, *sums)
     rest[3] = rest[3].T

time: 182 us -> 182 us (level)
  no operation moved by 1% of the time
where the time goes in v2:
time: 182 us
  Pallas kernels  181 us (99%)
    pallas_call x1, Pallas kernels, local(): pl.pallas_call(functools.partial(backward_kernel, heads, nt, nd, gathers)...  91.2 us
    pallas_call x1, Pallas kernels, local(): pl.pallas_call(functools.partial(forward_kernel, heads, nt, nd, gathers),...  84.8 us
    pallas_call x1, Pallas kernels, local(): pl.pallas_call(functools.partial(finish_kernel, nt, hloc), out_shape=[jax...  4.86 us

profile of v2, /device:TPU:0, one launch (start us, length us, event | category | flops | bytes accessed | tf_op | source)
XLA Modules:
  0.0 181.7 jit_solution(330915295880246216)
XLA Ops:
  0.7 84.8 %forward.1 = (bf16[1024,768]{1,0:T(8,128)(2,1)}, f32[2,528,1536]{2,1,0:T(8,128)}, f32[2,528,256]{2,1,0:T(8,128)}, bf16[1024,1536]{1,0:T(8,128)(2,1)}, bf16[1024,...) custom-call(bf16[1024,768]{1,0:T(8,128)(2,1)} %bitcast.8, ...), custom_call_target="tpu_custom_call" | custom-call | tf_op jit(solution)/shard_map/forward/pallas_call | solution.py:1527
  85.4 91.2 %backward.1 = (bf16[1024,768]{1,0:T(8,128)(2,1)}, bf16[1024,768]{1,0:T(8,128)(2,1)}, f32[96,384]{1,0:T(8,128)}, f32[96,384]{1,0:T(8,128)}, f32[96,384]{1,0:T(8,1...) custom-call(bf16[1024,768]{1,0:T(8,128)(2,1)} %bitcast.9, bf16[1024,768]{1,0:T(8,128)(2,1)} %bitcast.11, ...), custom_call_target="tpu_custom_call" | custom-call | tf_op jit(solution)/shard_map/backward/pallas_call | solution.py:1573
  176.6 4.9 %finish.1 = (bf16[1024,768]{1,0:T(8,128)(2,1)}, bf16[1024,768]{1,0:T(8,128)(2,1)}, f32[768]{0:T(1024)}, f32[96,2,384]{2,1,0:T(2,128)}, f32[96,256]{1,0:T(8,128)}...) custom-call(bf16[1024,768]{1,0:T(8,128)(2,1)} %get-tuple-element.93., ...), custom_call_target="tpu_custom_call" | custom-call | tf_op jit(solution)/shard_map/finish/pallas_call | solution.py:1591
